TPU v7x, 32 devices: a whole 2x2x4 slice. The times are simulated.
32 devices in a mesh: dp: 4 (over x, core), tensor: 8 (over z, y).
Axes of the slice: x: 2, y: 2, z: 4, core: 2. Of those that a mesh axis runs over, the one named last changes fastest.
Arguments:
- hidden_in: bfloat16 [4096, 4096], P(('dp', 'tensor')), parts along dimension 0, may hold values from -6 to 6
- norm_gain: bfloat16 [4096], replicated, may hold values from 0.099609375 to 1.8984375
- w_query: bfloat16 [4096, 4096], P(None, 'tensor'), may hold values from -0.09375 to 0.09375
- keyvalue_weight: bfloat16 [4096, 2048], P(None, 'tensor'), may hold values from -0.09375 to 0.09375
- w_out: bfloat16 [4096, 4096], P('tensor'), may hold values from -0.09375 to 0.09375
- prefix_keyvalue_cache: bfloat16 [4096, 2048], P(None, 'tensor'), may hold values from -600 to 600, as said below
- seg_ids: int32 [4096], P('dp'), parts along dimension 0, may hold values from 0 to 63, never falling along the last dimension, each value on 1 to 64 neighbouring positions
- seg_doc: int32 [256], P('dp'), parts along dimension 0, may hold values from 0 to 15
- doc_lens: int32 [16], replicated, may hold values from 1 to 1024, 4096 in all
Outputs:
- mixed: bfloat16 [4096, 4096], P(('dp', 'tensor')), parts along dimension 0
There are 4 independent parts, one for each index of `dp`. A program takes and returns all parts, laid end to end along the dimension named above; an argument that names none is the same for every part. Nothing has to cross between parts.
Inputs may be any that keep to these rules, and one draw needn't show every extreme that they name: `seg_ids`: segment numbers never fall along the tokens; each of the 64 samples holds 1 to 64 tokens, one exactly 64. `doc_lens`: the documents fill the prefix end to end in order, lengths summing to 4096, the longest exactly 1024. `prefix_keyvalue_cache`: cached keys already carry the rotary map of their prefix positions.
All inputs are finite; a program needn't handle non-finite values.
Results may differ from a plain program's by a relative error of at most 0.028.
The roundings to bfloat16 on the way count: a program that leaves them out, or rounds other values in their place, can miss the bound.
Values may be sent and summed in bfloat16 or wider, within the bound.
No kernel may reach another device: no remote copies, remote signals or barrier semaphores. Data moves between devices by JAX's collectives and lax.ppermute only.
A program may use at most 192 MiB of HBM per device.

v0:
```python
import functools
import math

import jax
import jax.numpy as jnp
import numpy as np
from jax import lax
from jax.experimental import pallas as pl
from jax.experimental.pallas import tpu as pltpu
from jax.sharding import PartitionSpec as P

HEAD = 128
TILE = 64
KEY_BLOCK = 256
GROUP = 4
MASKED = -1e30
EPS = 1e-05
ROPE_THETA = 500000.0
VMEM_LIMIT = 48 * 1024 * 1024


def ring_order(size):
    zs = 4 if size % 8 == 0 else 1
    ys = size // zs
    if zs == 1:
        return list(range(size))
    cycle = [(0, 0)]
    for y in range(ys):
        column = range(1, zs) if y % 2 == 0 else range(zs - 1, 0, -1)
        cycle += [(z, y) for z in column]
    cycle += [(0, y) for y in range(ys - 1, 0, -1)]
    return [z * ys + y for z, y in cycle]


def ready_tiles(order):
    size = len(order)
    place = {rank: i for i, rank in enumerate(order)}

    def distance(a, b):
        apart = (place[a] - place[b]) % size
        return min(apart, size - apart)

    steps = size // 2 + 1
    found = [[[] for _ in range(steps + 1)] for _ in range(size)]
    for rank in range(size):
        last = order[(place[rank] + size // 2) % size]
        for chunk in range(size):
            own = distance(rank, chunk)
            before = distance(rank, chunk - 1) if chunk else 0
            late = steps if max(own, before) == size // 2 and chunk != last else None
            first = max(own, before)
            found[rank][first if late is None else late].append(2 * chunk)
            found[rank][own].append(2 * chunk + 1)
    return found


def step_kernel(pieces, rows, heads, *refs):
    total = pieces * rows
    width = heads * HEAD
    it = iter(refs)
    ids, lists = next(it), next(it)
    xs = [next(it) for _ in range(pieces)]
    gain, wq, wkv, cos_tab, sin_tab, key_wide, cache, doc_bias, own_bias = [next(it) for _ in range(9)]
    first = pieces == 1 and rows == 128
    if not first:
        next(it), next(it), next(it)
    qb, kvb, att = next(it), next(it), next(it)
    (x_s, xn_s, wq_s, wkv_s, cos_s, sin_s, qo_s, kvo_s, key_s, val_s, qt_s, kvt_s, db_s, ob_s, sc_s, at_s,
     wide_s, own_s, m_s, l_s, o_s, sem_in, sem_tab, sem_w, sem_k, sem_out, sem_tile, sem_att) = list(it)
    blocks = key_wide.shape[0] - 1
    stride = blocks + GROUP

    key_copy = pltpu.make_async_copy(key_wide, key_s, sem_k.at[0])
    val_copy = pltpu.make_async_copy(cache.at[:, pl.ds(HEAD, HEAD)], val_s, sem_k.at[1])
    if pieces:
        x_copies, tab_copies = [], []
        for i in range(pieces):
            span = pl.ds(i * rows, rows)
            place = pl.ds(pl.multiple_of(ids[i] * TILE, TILE), rows)
            x_copies.append(pltpu.make_async_copy(xs[i], x_s.at[span], sem_in.at[i]))
            tab_copies.append(pltpu.make_async_copy(cos_tab.at[place], cos_s.at[span], sem_tab.at[2 * i]))
            tab_copies.append(pltpu.make_async_copy(sin_tab.at[place], sin_s.at[span], sem_tab.at[2 * i + 1]))
        for copy in x_copies:
            copy.start()
        w_copies = [
            pltpu.make_async_copy(wq.at[:, pl.ds(c, 256)], wq_s.at[:, pl.ds(c, 256)], sem_w.at[j])
            for j, c in enumerate(range(0, width, 256))
        ]
        w_copies.append(pltpu.make_async_copy(wkv, wkv_s, sem_w.at[len(w_copies)]))
        for copy in w_copies:
            copy.start()
        for copy in tab_copies:
            copy.start()
    key_copy.start()
    val_copy.start()

    if pieces:
        gains = gain[...]
        for i in range(pieces):
            x_copies[i].wait()

        def norm_rows(r, carry):
            span = pl.ds(pl.multiple_of(r * 16, 16), 16)
            values = x_s[span, :].astype(jnp.float32)
            mean_square = jnp.mean(values * values, axis=-1, keepdims=True)
            xn_s[span, :] = (values * lax.rsqrt(mean_square + EPS) * gains).astype(jnp.bfloat16)
            return carry

        lax.fori_loop(0, total // 16, norm_rows, 0, unroll=4)
        for copy in tab_copies:
            copy.wait()
        cosine, sine = cos_s[...], sin_s[...]

        def rotate(v):
            return (v * cosine + pltpu.roll(v, HEAD // 2, 1) * sine).astype(jnp.bfloat16)

        for j, c in enumerate(range(0, width, 256)):
            w_copies[j].wait()
            made = jnp.dot(xn_s[...], wq_s[:, c:c + 256], preferred_element_type=jnp.float32)
            for h in range(2):
                qo_s[c // HEAD + h] = rotate(made[:, h * HEAD:(h + 1) * HEAD])
        w_copies[-1].wait()
        made = jnp.dot(xn_s[...], wkv_s[...], preferred_element_type=jnp.float32)
        kvo_s[:, :HEAD] = rotate(made[:, :HEAD])
        kvo_s[:, HEAD:] = made[:, HEAD:].astype(jnp.bfloat16)
        outs = []
        for i in range(pieces):
            span = pl.ds(i * rows, rows)
            place = pl.ds(pl.multiple_of(ids[i] * TILE, TILE), rows)
            outs.append(pltpu.make_async_copy(qo_s.at[:, span], qb.at[:, place], sem_out.at[2 * i]))
            outs.append(pltpu.make_async_copy(kvo_s.at[span], kvb.at[place], sem_out.at[2 * i + 1]))
        for copy in outs:
            copy.start()
        for copy in outs:
            copy.wait()

    count = ids[2]
    factor = math.log2(math.e) / math.sqrt(HEAD)

    def fetches(i, slot):
        tile = ids[3 + i]
        at = pl.multiple_of(tile * TILE, TILE)
        before = pl.multiple_of(jnp.maximum(tile - 1, 0) * TILE, TILE)
        return [
            pltpu.make_async_copy(qb.at[:, pl.ds(at, TILE)], qt_s.at[slot], sem_tile.at[slot, 0]),
            pltpu.make_async_copy(kvb.at[pl.ds(before, 2 * TILE)], kvt_s.at[slot], sem_tile.at[slot, 1]),
            pltpu.make_async_copy(doc_bias.at[pl.ds(at, TILE)], db_s.at[slot], sem_tile.at[slot, 2]),
            pltpu.make_async_copy(own_bias.at[pl.ds(at, TILE)], ob_s.at[slot], sem_tile.at[slot, 3]),
        ]

    def att_copy(i):
        at = pl.multiple_of(ids[3 + i] * TILE, TILE)
        return pltpu.make_async_copy(at_s, att.at[pl.ds(at, TILE)], sem_att)

    @pl.when(count > 0)
    def _():
        for copy in fetches(0, 0):
            copy.start()

    key_copy.wait()
    val_copy.wait()
    contract_last = (((1,), (1,)), ((), ()))

    def one_tile(i, carry):
        slot = lax.rem(i, 2)

        @pl.when(i + 1 < count)
        def _():
            for copy in fetches(i + 1, 1 - slot):
                copy.start()

        for copy in fetches(i, slot):
            copy.wait()
        tile = ids[3 + i]
        needed = lists[tile * stride]
        for h in range(heads):
            wide_s[h * TILE:(h + 1) * TILE, :HEAD] = qt_s[slot, h]
            wide_s[h * TILE:(h + 1) * TILE, HEAD:] = db_s[slot]
        own = lax.dot_general(
            wide_s[:, :HEAD], kvt_s[slot, :, :HEAD], contract_last, preferred_element_type=jnp.float32
        )
        own = (own.reshape(heads, TILE, HEAD) + ob_s[slot][None]).reshape(heads * TILE, HEAD)
        own_s[...] = own
        m_s[...] = own

        def score_group(g, c):
            top_here = m_s[...]
            for u in range(GROUP):
                block = lists[tile * stride + 1 + g * GROUP + u]
                scores = jnp.dot(wide_s[...], key_s[block], preferred_element_type=jnp.float32)
                sc_s[g * GROUP + u] = scores
                top_here = jnp.maximum(top_here, jnp.maximum(scores[:, :HEAD], scores[:, HEAD:]))
            m_s[...] = top_here
            return c

        lax.fori_loop(0, needed, score_group, 0)
        top = jnp.max(m_s[...], axis=1, keepdims=True)
        weights = jnp.exp2((own_s[...] - top) * factor)
        l_s[...] = weights
        o_s[...] = jnp.dot(weights.astype(jnp.bfloat16), kvt_s[slot, :, HEAD:], preferred_element_type=jnp.float32)

        def value_group(g, c):
            total_here, sum_here = o_s[...], l_s[...]
            for u in range(GROUP):
                block = lists[tile * stride + 1 + g * GROUP + u]
                at = pl.multiple_of(jnp.minimum(block, blocks - 1) * KEY_BLOCK, KEY_BLOCK)
                weights = jnp.exp2((sc_s[g * GROUP + u] - top) * factor)
                sum_here = sum_here + (weights[:, :HEAD] + weights[:, HEAD:])
                total_here = total_here + jnp.dot(
                    weights.astype(jnp.bfloat16), val_s[pl.ds(at, KEY_BLOCK), :], preferred_element_type=jnp.float32
                )
            o_s[...] = total_here
            l_s[...] = sum_here
            return c

        lax.fori_loop(0, needed, value_group, 0)
        result = (o_s[...] / jnp.sum(l_s[...], axis=1, keepdims=True)).astype(jnp.bfloat16)

        @pl.when(i > 0)
        def _():
            att_copy(i - 1).wait()

        for h in range(heads):
            at_s[:, h * HEAD:(h + 1) * HEAD] = result[h * TILE:(h + 1) * TILE]
        att_copy(i).start()
        return carry

    lax.fori_loop(0, count, one_tile, 0)

    @pl.when(count > 0)
    def _():
        att_copy(count - 1).wait()


def run_step(ids, lists, xs, fixed, state, dims):
    tokens, heads, prefix, depth = dims
    pieces = len(xs)
    rows = xs[0].shape[0] if pieces else TILE
    total = max(pieces * rows, 16)
    width = heads * HEAD
    any_spec = pl.BlockSpec(memory_space=pl.ANY)
    vmem_spec = pl.BlockSpec(memory_space=pltpu.VMEM)
    operands = list(xs) + list(fixed)
    specs = [any_spec] * pieces + [vmem_spec] + [any_spec] * (len(fixed) - 1)
    aliases = {}
    if state is not None:
        aliases = {2 + len(operands) + i: i for i in range(3)}
        operands += list(state)
        specs += [any_spec] * 3
    out_shape = [
        jax.ShapeDtypeStruct((heads, tokens, HEAD), jnp.bfloat16),
        jax.ShapeDtypeStruct((tokens, 2 * HEAD), jnp.bfloat16),
        jax.ShapeDtypeStruct((tokens, width), jnp.bfloat16),
    ]
    small = 16
    w_rows = depth if pieces else small
    scratch = [
        pltpu.VMEM((total, depth), jnp.bfloat16),
        pltpu.VMEM((total, depth), jnp.bfloat16),
        pltpu.VMEM((w_rows, width), jnp.bfloat16),
        pltpu.VMEM((w_rows, 2 * HEAD), jnp.bfloat16),
        pltpu.VMEM((total, HEAD), jnp.float32),
        pltpu.VMEM((total, HEAD), jnp.float32),
        pltpu.VMEM((heads, total, HEAD), jnp.bfloat16),
        pltpu.VMEM((total, 2 * HEAD), jnp.bfloat16),
        pltpu.VMEM((prefix // KEY_BLOCK + 1, 2 * HEAD, KEY_BLOCK), jnp.bfloat16),
        pltpu.VMEM((prefix, HEAD), jnp.bfloat16),
        pltpu.VMEM((2, heads, TILE, HEAD), jnp.bfloat16),
        pltpu.VMEM((2, 2 * TILE, 2 * HEAD), jnp.bfloat16),
        pltpu.VMEM((2, TILE, HEAD), jnp.bfloat16),
        pltpu.VMEM((2, TILE, HEAD), jnp.float32),
        pltpu.VMEM((prefix // KEY_BLOCK, heads * TILE, KEY_BLOCK), jnp.float32),
        pltpu.VMEM((TILE, width), jnp.bfloat16),
        pltpu.VMEM((heads * TILE, 2 * HEAD), jnp.bfloat16),
        pltpu.VMEM((heads * TILE, HEAD), jnp.float32),
        pltpu.VMEM((heads * TILE, HEAD), jnp.float32),
        pltpu.VMEM((heads * TILE, HEAD), jnp.float32),
        pltpu.VMEM((heads * TILE, HEAD), jnp.float32),
        pltpu.SemaphoreType.DMA((max(pieces, 1),)),
        pltpu.SemaphoreType.DMA((2 * max(pieces, 1),)),
        pltpu.SemaphoreType.DMA((width // 256 + 1,)),
        pltpu.SemaphoreType.DMA((2,)),
        pltpu.SemaphoreType.DMA((2 * max(pieces, 1),)),
        pltpu.SemaphoreType.DMA((2, 4)),
        pltpu.SemaphoreType.DMA,
    ]
    flops = 2 * pieces * rows * depth * (width + 256) + 2 * 2 * 2 * TILE * width * prefix
    return pl.pallas_call(
        functools.partial(step_kernel, pieces, rows, heads),
        grid_spec=pltpu.PrefetchScalarGridSpec(
            num_scalar_prefetch=2,
            grid=(),
            in_specs=specs,
            out_specs=[any_spec] * 3,
            scratch_shapes=scratch,
        ),
        out_shape=out_shape,
        input_output_aliases=aliases,
        compiler_params=pltpu.CompilerParams(vmem_limit_bytes=VMEM_LIMIT),
        cost_estimate=pl.CostEstimate(flops=flops, bytes_accessed=12 << 20, transcendentals=0),
    )(ids, lists, *operands)


def send_kernel(has, shared, *refs):
    count = len(has)
    rest = iter(refs[1:])
    atts = [next(rest) for _ in range(count)]
    weights = [next(rest)] * count if shared else [next(rest) for _ in range(count)]
    arrived = [[next(rest) for _ in range(many)] for many in has]
    outs = refs[-count:]
    for i in range(count):
        made = jnp.dot(atts[i][...], weights[i][...], preferred_element_type=jnp.float32)
        made = made.astype(jnp.bfloat16).astype(jnp.float32)
        for other in arrived[i]:
            made = made + other[...].astype(jnp.float32)
        outs[i][...] = made.astype(jnp.bfloat16)


def run_send(ids, att, w_out, arrived, pieces, chunk_rows, columns):
    count = len(arrived)
    block = 512
    per_piece = columns // block
    width = att.shape[1]
    shared = len(set(pieces)) == 1
    used = pieces[:1] if shared else pieces
    row_block = pl.BlockSpec((chunk_rows, block), lambda b, ids: (0, b))
    in_specs = [pl.BlockSpec((chunk_rows, width), lambda b, ids, i=i: (ids[i], 0)) for i in range(count)]
    in_specs += [pl.BlockSpec((width, block), lambda b, ids, p=p: (0, p * per_piece + b)) for p in used]
    operands = [att] * count + [w_out] * len(used)
    for group in arrived:
        operands += group
        in_specs += [row_block] * len(group)
    return pl.pallas_call(
        functools.partial(send_kernel, [len(group) for group in arrived], shared),
        grid_spec=pltpu.PrefetchScalarGridSpec(
            num_scalar_prefetch=1, grid=(per_piece,), in_specs=in_specs, out_specs=[row_block] * count
        ),
        out_shape=[jax.ShapeDtypeStruct((chunk_rows, columns), jnp.bfloat16)] * count,
        compiler_params=pltpu.CompilerParams(vmem_limit_bytes=VMEM_LIMIT),
        cost_estimate=pl.CostEstimate(
            flops=2 * count * chunk_rows * width * columns, bytes_accessed=4 << 20, transcendentals=0
        ),
    )(ids, *operands)


def tables(seg_ids, seg_doc, doc_lens, prefix, cache):
    tokens = seg_ids.shape[0]
    tiles = tokens // TILE
    blocks = prefix // KEY_BLOCK
    docs = doc_lens.shape[0]
    order = jnp.arange(tokens, dtype=jnp.int32)
    start = jnp.sum((seg_ids[None, :] < seg_ids[:, None]).astype(jnp.int32), axis=1, dtype=jnp.int32)
    positions = prefix + order - start
    segments = jnp.arange(seg_doc.shape[0], dtype=jnp.int32)
    tok_doc = jnp.sum(
        jnp.where(seg_ids[:, None] == segments[None, :], seg_doc[None, :], 0), axis=1, dtype=jnp.int32
    )
    doc_list = jnp.arange(docs, dtype=jnp.int32)
    doc_ends = jnp.sum(jnp.where(doc_list[None, :] <= doc_list[:, None], doc_lens[None, :], 0), axis=1)
    doc_starts = doc_ends - doc_lens
    lanes = jnp.arange(HEAD, dtype=jnp.int32)
    half = HEAD // 2
    inverse = ROPE_THETA ** (-(jnp.arange(half, dtype=jnp.float32) * 2.0 / HEAD))
    inverse = jnp.concatenate([inverse, inverse])
    angles = positions.astype(jnp.float32)[:, None] * inverse[None, :]
    cosine = jnp.cos(angles)
    sine = jnp.sin(angles) * jnp.where(lanes < half, -1.0, 1.0)[None, :]
    doc_bias = jnp.where(lanes[None, :] == tok_doc[:, None], 0.0, MASKED).astype(jnp.bfloat16)
    spot = jnp.arange(prefix + KEY_BLOCK, dtype=jnp.int32).reshape(blocks + 1, 1, KEY_BLOCK)
    low = jnp.pad(doc_starts, (0, HEAD - docs), constant_values=prefix).reshape(1, HEAD, 1)
    high = jnp.pad(doc_ends, (0, HEAD - docs), constant_values=prefix + KEY_BLOCK).reshape(1, HEAD, 1)
    one_hot = ((spot >= low) & (spot < high)).astype(jnp.bfloat16)
    by_block = cache[:, :HEAD].reshape(blocks, KEY_BLOCK, HEAD).transpose(0, 2, 1)
    key_wide = jnp.concatenate([jnp.pad(by_block, ((0, 1), (0, 0), (0, 0))), one_hot], axis=1)
    first_key = jnp.maximum(jnp.arange(tiles, dtype=jnp.int32) - 1, 0) * TILE
    spots = first_key[:, None] + lanes[None, :]
    by_tile = seg_ids.reshape(tiles, TILE)
    earlier = jnp.concatenate([by_tile[:1], by_tile[:-1]], axis=0)
    later = jnp.concatenate([by_tile[1:2], by_tile[1:]], axis=0)
    window_seg = jnp.concatenate([earlier, later], axis=1)
    ok = (window_seg[:, None, :] == by_tile[:, :, None]) & (
        spots[:, None, :] <= order.reshape(tiles, TILE)[:, :, None]
    )
    own_bias = jnp.where(ok, 0.0, MASKED).astype(jnp.float32).reshape(tokens, HEAD)
    present = jnp.any(tok_doc.reshape(tiles, TILE)[:, :, None] == doc_list[None, None, :], axis=1)
    edge = jnp.arange(blocks, dtype=jnp.int32) * KEY_BLOCK
    overlap = (doc_starts[:, None] < edge[None, :] + KEY_BLOCK) & (doc_ends[:, None] > edge[None, :])
    flags = jnp.any(present[:, :, None] & overlap[None, :, :], axis=1).astype(jnp.int32)
    block_ids = jnp.arange(blocks, dtype=jnp.int32)
    rank = jnp.sum(jnp.where(block_ids[None, :, None] > block_ids[None, None, :], flags[:, None, :], 0), axis=2)
    listed = jnp.sum(
        jnp.where((rank[:, :, None] == block_ids[None, None, :]) & (flags[:, :, None] > 0), block_ids[None, :, None], 0),
        axis=1,
    )
    count = jnp.sum(flags, axis=1, keepdims=True)
    listed = jnp.where(block_ids[None, :] < count, listed, blocks)
    groups = (count + GROUP - 1) // GROUP
    lists = jnp.pad(jnp.concatenate([groups, listed], axis=1), ((0, 0), (0, GROUP - 1)))
    lists = lists.astype(jnp.int32).reshape(-1)
    return cosine, sine, key_wide, doc_bias, own_bias, lists


def local(
    hidden_in, norm_gain, w_query, keyvalue_weight, w_out, prefix_keyvalue_cache, seg_ids, seg_doc, doc_lens
):
    size = lax.axis_size("tensor")
    tokens = seg_ids.shape[0]
    prefix = prefix_keyvalue_cache.shape[0]
    chunk_rows, depth = hidden_in.shape
    heads = w_query.shape[1] // HEAD
    order = ring_order(size)
    half = size // 2
    rank = lax.axis_index("tensor")

    forward_pairs = [(order[i], order[(i + 1) % size]) for i in range(size)]
    backward_pairs = [(b, a) for a, b in forward_pairs]

    def forward(x):
        return lax.ppermute(x, "tensor", forward_pairs)

    def backward(x):
        return lax.ppermute(x, "tensor", backward_pairs)

    if keyvalue_weight.shape[1] == HEAD:
        swap = [(i, i ^ 1) for i in range(size)]
        even = rank % 2 == 0
        other_weight, other_cache = lax.ppermute((keyvalue_weight, prefix_keyvalue_cache), "tensor", swap)
        keyvalue_weight = jnp.concatenate(
            [jnp.where(even, keyvalue_weight, other_weight), jnp.where(even, other_weight, keyvalue_weight)], axis=1
        )
        prefix_keyvalue_cache = jnp.concatenate(
            [
                jnp.where(even, prefix_keyvalue_cache, other_cache),
                jnp.where(even, other_cache, prefix_keyvalue_cache),
            ],
            axis=1,
        )

    place = {r: i for i, r in enumerate(order)}
    around = np.array([[order[(place[r] + d) % size] for d in range(size)] for r in range(size)], np.int32)
    ready = ready_tiles(order)
    most = max(len(ready[r][s]) for r in range(size) for s in range(half + 2))
    plan = np.zeros((size, half + 2, 3 + most), np.int32)
    for r in range(size):
        for s in range(half + 2):
            ids = [0, 0]
            if s < half:
                ids = [2 * around[r][(-s) % size], 2 * around[r][s]]
            elif s == half:
                ids = [2 * around[r][half], 2 * around[r][half] + 1]
            row = ids + [len(ready[r][s])] + ready[r][s]
            plan[r, s, :len(row)] = row
    my_plan = jnp.asarray(plan)[rank]
    my_around = jnp.asarray(around)[rank]

    cosine, sine, key_wide, doc_bias, own_bias, lists = tables(
        seg_ids, seg_doc, doc_lens, prefix, prefix_keyvalue_cache
    )
    gain = norm_gain.astype(jnp.float32).reshape(1, depth)
    fixed = (gain, w_query, keyvalue_weight, cosine, sine, key_wide, prefix_keyvalue_cache, doc_bias, own_bias)
    dims = (tokens, heads, prefix, depth)

    from_left, from_right = hidden_in, hidden_in
    state = None
    held = [hidden_in]
    for s in range(half):
        if s + 1 < half:
            next_left, next_right = forward(from_left), backward(from_right)
        else:
            next_left, next_right = forward(from_left[:TILE]), backward(from_right[TILE:])
        state = run_step(my_plan[s], lists, held, fixed, state, dims)
        (next_left, next_right), state = lax.optimization_barrier(((next_left, next_right), tuple(state)))
        from_left, from_right = next_left, next_right
        held = [from_left, from_right]
    state = run_step(my_plan[half], lists, held, fixed, state, dims)
    columns = depth // 2

    def ids_of(*distances):
        return jnp.stack([my_around[d % size] for d in distances])

    sent = run_send(ids_of(half, half), state[2], w_out, [[], []], [0, 1], chunk_rows, columns)
    sent, state = lax.optimization_barrier((tuple(sent), tuple(state)))
    arrived = [[[forward(sent[0])], []], [[], [backward(sent[1])]]]
    att = run_step(my_plan[half + 1], lists, [], fixed, state, dims)[2]
    for d in range(half - 1, 0, -1):
        following = []
        for piece in range(2):
            made = run_send(ids_of(d, -d), att, w_out, arrived[piece], [piece, piece], chunk_rows, columns)
            following.append([[forward(made[0])], [backward(made[1])]])
        arrived = following
    own = run_send(ids_of(0), att, w_out, [[]], [0], chunk_rows, depth)[0]
    result = hidden_in.astype(jnp.float32) + own.astype(jnp.float32)
    (left_0,), (right_0,) = arrived[0]
    (left_1,), (right_1,) = arrived[1]
    summed = jnp.concatenate(
        [left.astype(jnp.float32) + right.astype(jnp.float32) for left, right in ((left_0, right_0), (left_1, right_1))],
        axis=1,
    )
    return (result + summed).astype(jnp.bfloat16)


def solution(mesh):
    return jax.shard_map(
        local,
        mesh=mesh,
        in_specs=(
            P(("dp", "tensor"), None),
            P(),
            P(None, "tensor"),
            P(None, "tensor"),
            P("tensor", None),
            P(None, "tensor"),
            P("dp"),
            P("dp"),
            P(),
        ),
        out_specs=P(("dp", "tensor"), None),
        check_vma=False,
    )
```

profile of v0, /device:TPU:0, one launch (start us, length us, event | category | flops | bytes accessed | tf_op | source)
XLA Modules:
  0.0 195.8 jit_solution(3225787413182336350)
XLA Ops:
  0.0 3.0 %collective-permute-start = (bf16[128,4096]{1,0:T(8,128)(2,1)}, bf16[128,4096]{1,0:T(8,128)(2,1)S(1)}, u32[]{:S(2)}, u32[]{:S(2)}) collective-permute-start(bf16[128,4096]{1,0:T(8,128)(2,1)} %refs_2_.2), channel_id=1, source_target_pairs={{0,2},{2,4},{4,6},{6,7},{7,5},{5,3},{3,1},{1,0},{8,10},{10,12},{12... | collective-permute-start | bytes 3145736 | tf_op jit(solution)/shard_map/ppermute | solution.py:419
  3.0 0.8 select_reduce_fusion.3
  4.5 0.8 select_reduce_fusion
  6.0 0.8 fusion.11
  6.9 0.8 slice_bitcast_fusion.6
  9.3 1.3 copy.34
  11.2 2.9 %fusion.1.refs_8_.refs_9_.refs_7_ = bf16[17,256,256]{2,1,0:T(8,128)(2,1)} fusion(bf16[16,128,256]{2,1,0:T(8,128)(2,1)} %bitcast.46, bf16[17,128,256]{2,1,0:T(8,128)(2,1)S(1)} %and_convert_fusion), kind=kLoop, calls=%fused_computation.3 | loop fusion | flops 6684672 | bytes 4390912 | tf_op jit(solution)/shard_map/concatenate | solution.py:374
  15.6 1.9 fusion.3
  17.5 8.8 %shard_map.109 = (bf16[4,1024,128]{2,1,0:T(8,128)(2,1)S(1)}, bf16[1024,256]{1,0:T(8,128)(2,1)S(1)}, bf16[1024,512]{1,0:T(8,128)(2,1)S(1)}) custom-call(s32[9]{0:T(128)S(1)} %get-tuple-element.120.refs_0_, s32[320]{0:T(512)S(1)} %reshape.302.refs_1_, bf16[128,4096]{1,0:T(8,128)(2,1)S(1)} %copy-done, f32[1,4096]{1,0:T(1,128)S(1)} %bitcast.39, ...), custom_call_target="tpu_custom_call" | custom-call | flops 1879048192 | bytes 12582912 | tf_op jit(solution)/shard_map/pallas_call | solution.py:288
  26.3 1.6 collective-permute-done.1.refs_3_
  28.0 1.6 collective-permute-start.2
  30.0 18.1 %shard_map.110 = (bf16[4,1024,128]{2,1,0:T(8,128)(2,1)S(1)}, bf16[1024,256]{1,0:T(8,128)(2,1)S(1)}, bf16[1024,512]{1,0:T(8,128)(2,1)S(1)}) custom-call(s32[9]{0:T(128)S(1)} %get-tuple-element.119.refs_0_, s32[320]{0:T(512)S(1)} %reshape.302.refs_1_, ...), custom_call_target="tpu_custom_call", output_to_operand_aliasing={{0}: (13, {}), {1}: (14, {}), {2}: (15, {})} | custom-call | flops 2684354560 | bytes 12582912 | tf_op jit(solution)/shard_map/pallas_call | solution.py:288
  48.1 3.6 %collective-permute-done.2.refs_2_ = bf16[128,4096]{1,0:T(8,128)(2,1)S(1)} collective-permute-done((bf16[128,4096]{1,0:T(8,128)(2,1)S(1)}, bf16[128,4096]{1,0:T(8,128)(2,1)S(1)}, u32[]{:S(2)}, u32[]{:S(2)}) %collective-permute-start.2) | collective-permute-done | bytes 1048608 | tf_op jit(solution)/shard_map/ppermute | solution.py:419
  51.7 1.5 collective-permute-done.3.refs_3_
  53.2 1.6 collective-permute-start.4
  55.2 17.5 %shard_map.111 = (bf16[4,1024,128]{2,1,0:T(8,128)(2,1)S(1)}, bf16[1024,256]{1,0:T(8,128)(2,1)S(1)}, bf16[1024,512]{1,0:T(8,128)(2,1)S(1)}) custom-call(s32[9]{0:T(128)S(1)} %get-tuple-element.118.refs_0_, s32[320]{0:T(512)S(1)} %reshape.302.refs_1_, ...), custom_call_target="tpu_custom_call", output_to_operand_aliasing={{0}: (13, {}), {1}: (14, {}), {2}: (15, {})} | custom-call | flops 2684354560 | bytes 12582912 | tf_op jit(solution)/shard_map/pallas_call | solution.py:288
  72.7 3.0 %collective-permute-done.4.refs_2_ = bf16[128,4096]{1,0:T(8,128)(2,1)S(1)} collective-permute-done((bf16[128,4096]{1,0:T(8,128)(2,1)S(1)}, bf16[128,4096]{1,0:T(8,128)(2,1)S(1)}, u32[]{:S(2)}, u32[]{:S(2)}) %collective-permute-start.4) | collective-permute-done | bytes 1048608 | tf_op jit(solution)/shard_map/ppermute | solution.py:419
  75.7 1.3 collective-permute-done.5.refs_3_
  77.0 1.9 collective-permute-start.6
  81.2 18.7 %shard_map.112 = (bf16[4,1024,128]{2,1,0:T(8,128)(2,1)S(1)}, bf16[1024,256]{1,0:T(8,128)(2,1)S(1)}, bf16[1024,512]{1,0:T(8,128)(2,1)S(1)}) custom-call(s32[9]{0:T(128)S(1)} %get-tuple-element.117.refs_0_, s32[320]{0:T(512)S(1)} %reshape.302.refs_1_, ...), custom_call_target="tpu_custom_call", output_to_operand_aliasing={{0}: (13, {}), {1}: (14, {}), {2}: (15, {})} | custom-call | flops 2684354560 | bytes 12582912 | tf_op jit(solution)/shard_map/pallas_call | solution.py:288
  100.0 9.5 %shard_map.113 = (bf16[4,1024,128]{2,1,0:T(8,128)(2,1)S(1)}, bf16[1024,256]{1,0:T(8,128)(2,1)S(1)}, bf16[1024,512]{1,0:T(8,128)(2,1)S(1)}) custom-call(s32[9]{0:T(128)S(1)} %get-tuple-element.121.refs_0_, s32[320]{0:T(512)S(1)} %reshape.302.refs_1_, ...), custom_call_target="tpu_custom_call", output_to_operand_aliasing={{0}: (13, {}), {1}: (14, {}), {2}: (15, {})} | custom-call | flops 1879048192 | bytes 12582912 | tf_op jit(solution)/shard_map/pallas_call | solution.py:288
  109.5 4.1 %shard_map.114 = (bf16[128,2048]{1,0:T(8,128)(2,1)S(1)}, bf16[128,2048]{1,0:T(8,128)(2,1)S(1)}) custom-call(s32[2]{0:T(128)S(1)} %pad_add_fusion.1.refs_0_, bf16[1024,512]{1,0:T(8,128)(2,1)S(1)} %get-tuple-element.99.refs_1_.refs_2_.refs_13_, bf16[1024,512]{1,0:T(8,128)(2,1)S(1)} %get-tuple-element.99.refs_1_.refs_2_.refs_13_, bf16[512,4096]{1,0:T(8,128)(2,1)} %refs_3_.15, ...), custom_call_target="tpu_custom_call" | custom-call | flops 536870912 | bytes 4194304 | tf_op jit(solution)/shard_map/pallas_call | solution.py:333
  113.6 2.0 %collective-permute-start.8 = (bf16[128,2048]{1,0:T(8,128)(2,1)S(1)}, bf16[128,2048]{1,0:T(8,128)(2,1)S(1)}, u32[]{:S(2)}, u32[]{:S(2)}) collective-permute-start(bf16[128,2048]{1,0:T(8,128)(2,1)S(1)} %get-tuple-element.101), channel_id=1, source_target_pairs={{0,2},{2,4},{4,6},{6,7},{7,5},{5,3},{3,1},{1,0},{8,10},{10,12},{12... | collective-permute-start | bytes 1572872 | tf_op jit(solution)/shard_map/ppermute | solution.py:419
  115.7 1.3 pad_add_fusion.4.refs_0_
  117.0 2.6 %shard_map.115 = (bf16[4,1024,128]{2,1,0:T(8,128)(2,1)S(1)}, bf16[1024,256]{1,0:T(8,128)(2,1)S(1)}, bf16[1024,512]{1,0:T(8,128)(2,1)S(1)}) custom-call(s32[9]{0:T(128)S(1)} %get-tuple-element.122.refs_0_, s32[320]{0:T(512)S(1)} %reshape.302.refs_1_, f32[1,4096]{1,0:T(1,128)S(1)} %bitcast.44, ...), custom_call_target="tpu_custom_call", output_to_operand_aliasing={{0}: (11, {}), {1}: (12, {}), {2}: (13, {})} | custom-call | flops 1073741824 | bytes 12582912 | tf_op jit(solution)/shard_map/pallas_call | solution.py:288
  119.7 3.4 %collective-permute-done.8.refs_4_ = bf16[128,2048]{1,0:T(8,128)(2,1)S(1)} collective-permute-done((bf16[128,2048]{1,0:T(8,128)(2,1)S(1)}, bf16[128,2048]{1,0:T(8,128)(2,1)S(1)}, u32[]{:S(2)}, u32[]{:S(2)}) %collective-permute-start.8) | collective-permute-done | bytes 524320 | tf_op jit(solution)/shard_map/ppermute | solution.py:419
  123.0 3.7 %shard_map.117 = (bf16[128,2048]{1,0:T(8,128)(2,1)S(1)}, bf16[128,2048]{1,0:T(8,128)(2,1)S(1)}) custom-call(s32[2]{0:T(128)S(1)} %pad_add_fusion.4.refs_0_, bf16[1024,512]{1,0:T(8,128)(2,1)S(1)} %get-tuple-element.100.refs_1_.refs_2_, bf16[1024,512]{1,0:T(8,128)(2,1)S(1)} %get-tuple-element.100.refs_1_.refs_2_, bf16[512,4096]{1,0:T(8,128)(2,1)} %refs_3_.15, ...), custom_call_target="tpu_custom_call" | custom-call | flops 536870912 | bytes 4194304 | tf_op jit(solution)/shard_map/pallas_call | solution.py:333
  126.7 3.5 %collective-permute-start.10 = (bf16[128,2048]{1,0:T(8,128)(2,1)S(1)}, bf16[128,2048]{1,0:T(8,128)(2,1)S(1)}, u32[]{:S(2)}, u32[]{:S(2)}) collective-permute-start(bf16[128,2048]{1,0:T(8,128)(2,1)S(1)} %get-tuple-element.103), channel_id=1, source_target_pairs={{2,0},{4,2},{6,4},{7,6},{5,7},{3,5},{1,3},{0,1},{10,8},{12,10},{14... | collective-permute-start | bytes 1572872 | tf_op jit(solution)/shard_map/ppermute | solution.py:422
  130.2 3.7 %shard_map.120 = (bf16[128,2048]{1,0:T(8,128)(2,1)S(1)}, bf16[128,2048]{1,0:T(8,128)(2,1)S(1)}) custom-call(s32[2]{0:T(128)S(1)} %pad_add_fusion.4.refs_0_, bf16[1024,512]{1,0:T(8,128)(2,1)S(1)} %get-tuple-element.100.refs_1_.refs_2_, bf16[1024,512]{1,0:T(8,128)(2,1)S(1)} %get-tuple-element.100.refs_1_.refs_2_, bf16[512,4096]{1,0:T(8,128)(2,1)} %refs_3_.15, ...), custom_call_target="tpu_custom_call" | custom-call | flops 536870912 | bytes 4194304 | tf_op jit(solution)/shard_map/pallas_call | solution.py:333
  134.0 2.1 %collective-permute-start.16 = (bf16[128,2048]{1,0:T(8,128)(2,1)S(1)}, bf16[128,2048]{1,0:T(8,128)(2,1)S(1)}, u32[]{:S(2)}, u32[]{:S(2)}) collective-permute-start(bf16[128,2048]{1,0:T(8,128)(2,1)S(1)} %get-tuple-element.109), channel_id=1, source_target_pairs={{0,2},{2,4},{4,6},{6,7},{7,5},{5,3},{3,1},{1,0},{8,10},{10,12},{12... | collective-permute-start | bytes 1572872 | tf_op jit(solution)/shard_map/ppermute | solution.py:419
  136.1 1.4 pad_add_fusion.3.refs_0_
  137.5 5.1 %collective-permute-done.10.refs_5_ = bf16[128,2048]{1,0:T(8,128)(2,1)S(1)} collective-permute-done((bf16[128,2048]{1,0:T(8,128)(2,1)S(1)}, bf16[128,2048]{1,0:T(8,128)(2,1)S(1)}, u32[]{:S(2)}, u32[]{:S(2)}) %collective-permute-start.10) | collective-permute-done | bytes 524320 | tf_op jit(solution)/shard_map/ppermute | solution.py:422
  142.6 2.5 %collective-permute-done.9.refs_4_ = bf16[128,2048]{1,0:T(8,128)(2,1)S(1)} collective-permute-done((bf16[128,2048]{1,0:T(8,128)(2,1)S(1)}, bf16[128,2048]{1,0:T(8,128)(2,1)S(1)}, u32[]{:S(2)}, u32[]{:S(2)}) %collective-permute-start.9) | collective-permute-done | bytes 524320 | tf_op jit(solution)/shard_map/ppermute | solution.py:419
  145.1 3.7 %shard_map.118 = (bf16[128,2048]{1,0:T(8,128)(2,1)S(1)}, bf16[128,2048]{1,0:T(8,128)(2,1)S(1)}) custom-call(s32[2]{0:T(128)S(1)} %pad_add_fusion.3.refs_0_, bf16[1024,512]{1,0:T(8,128)(2,1)S(1)} %get-tuple-element.100.refs_1_.refs_2_, bf16[1024,512]{1,0:T(8,128)(2,1)S(1)} %get-tuple-element.100.refs_1_.refs_2_, bf16[512,4096]{1,0:T(8,128)(2,1)} %refs_3_.15, ...), custom_call_target="tpu_custom_call" | custom-call | flops 536870912 | bytes 4194304 | tf_op jit(solution)/shard_map/pallas_call | solution.py:333
  148.9 2.1 %collective-permute-start.12 = (bf16[128,2048]{1,0:T(8,128)(2,1)S(1)}, bf16[128,2048]{1,0:T(8,128)(2,1)S(1)}, u32[]{:S(2)}, u32[]{:S(2)}) collective-permute-start(bf16[128,2048]{1,0:T(8,128)(2,1)S(1)} %get-tuple-element.105), channel_id=1, source_target_pairs={{2,0},{4,2},{6,4},{7,6},{5,7},{3,5},{1,3},{0,1},{10,8},{12,10},{14... | collective-permute-start | bytes 1572872 | tf_op jit(solution)/shard_map/ppermute | solution.py:422
  150.9 5.4 %collective-permute-done.16.refs_4_ = bf16[128,2048]{1,0:T(8,128)(2,1)S(1)} collective-permute-done((bf16[128,2048]{1,0:T(8,128)(2,1)S(1)}, bf16[128,2048]{1,0:T(8,128)(2,1)S(1)}, u32[]{:S(2)}, u32[]{:S(2)}) %collective-permute-start.16) | collective-permute-done | bytes 524320 | tf_op jit(solution)/shard_map/ppermute | solution.py:419
  156.3 3.7 %shard_map.121 = (bf16[128,2048]{1,0:T(8,128)(2,1)S(1)}, bf16[128,2048]{1,0:T(8,128)(2,1)S(1)}) custom-call(s32[2]{0:T(128)S(1)} %pad_add_fusion.3.refs_0_, bf16[1024,512]{1,0:T(8,128)(2,1)S(1)} %get-tuple-element.100.refs_1_.refs_2_, bf16[1024,512]{1,0:T(8,128)(2,1)S(1)} %get-tuple-element.100.refs_1_.refs_2_, bf16[512,4096]{1,0:T(8,128)(2,1)} %refs_3_.15, ...), custom_call_target="tpu_custom_call" | custom-call | flops 536870912 | bytes 4194304 | tf_op jit(solution)/shard_map/pallas_call | solution.py:333
  160.1 2.1 %collective-permute-start.19 = (bf16[128,2048]{1,0:T(8,128)(2,1)S(1)}, bf16[128,2048]{1,0:T(8,128)(2,1)S(1)}, u32[]{:S(2)}, u32[]{:S(2)}) collective-permute-start(bf16[128,2048]{1,0:T(8,128)(2,1)S(1)} %get-tuple-element.112), channel_id=1, source_target_pairs={{2,0},{4,2},{6,4},{7,6},{5,7},{3,5},{1,3},{0,1},{10,8},{12,10},{14... | collective-permute-start | bytes 1572872 | tf_op jit(solution)/shard_map/ppermute | solution.py:422
  162.2 1.4 pad_add_fusion.2.refs_0_
  163.7 3.9 %collective-permute-done.11.refs_4_ = bf16[128,2048]{1,0:T(8,128)(2,1)S(1)} collective-permute-done((bf16[128,2048]{1,0:T(8,128)(2,1)S(1)}, bf16[128,2048]{1,0:T(8,128)(2,1)S(1)}, u32[]{:S(2)}, u32[]{:S(2)}) %collective-permute-start.11) | collective-permute-done | bytes 524320 | tf_op jit(solution)/shard_map/ppermute | solution.py:419
  167.6 3.7 %shard_map.119 = (bf16[128,2048]{1,0:T(8,128)(2,1)S(1)}, bf16[128,2048]{1,0:T(8,128)(2,1)S(1)}) custom-call(s32[2]{0:T(128)S(1)} %pad_add_fusion.2.refs_0_, bf16[1024,512]{1,0:T(8,128)(2,1)S(1)} %get-tuple-element.100.refs_1_.refs_2_, bf16[1024,512]{1,0:T(8,128)(2,1)S(1)} %get-tuple-element.100.refs_1_.refs_2_, bf16[512,4096]{1,0:T(8,128)(2,1)} %refs_3_.15, ...), custom_call_target="tpu_custom_call" | custom-call | flops 536870912 | bytes 4194304 | tf_op jit(solution)/shard_map/pallas_call | solution.py:333
  171.3 2.1 %collective-permute-start.14 = (bf16[128,2048]{1,0:T(8,128)(2,1)S(1)}, bf16[128,2048]{1,0:T(8,128)(2,1)S(1)}, u32[]{:S(2)}, u32[]{:S(2)}) collective-permute-start(bf16[128,2048]{1,0:T(8,128)(2,1)S(1)} %get-tuple-element.107), channel_id=1, source_target_pairs={{2,0},{4,2},{6,4},{7,6},{5,7},{3,5},{1,3},{0,1},{10,8},{12,10},{14... | collective-permute-start | bytes 1572872 | tf_op jit(solution)/shard_map/ppermute | solution.py:422
  173.4 5.4 %collective-permute-done.18.refs_4_ = bf16[128,2048]{1,0:T(8,128)(2,1)S(1)} collective-permute-done((bf16[128,2048]{1,0:T(8,128)(2,1)S(1)}, bf16[128,2048]{1,0:T(8,128)(2,1)S(1)}, u32[]{:S(2)}, u32[]{:S(2)}) %collective-permute-start.18) | collective-permute-done | bytes 524320 | tf_op jit(solution)/shard_map/ppermute | solution.py:419
  178.8 3.7 %shard_map.122 = (bf16[128,2048]{1,0:T(8,128)(2,1)S(1)}, bf16[128,2048]{1,0:T(8,128)(2,1)S(1)}) custom-call(s32[2]{0:T(128)S(1)} %pad_add_fusion.2.refs_0_, bf16[1024,512]{1,0:T(8,128)(2,1)S(1)} %get-tuple-element.100.refs_1_.refs_2_, bf16[1024,512]{1,0:T(8,128)(2,1)S(1)} %get-tuple-element.100.refs_1_.refs_2_, bf16[512,4096]{1,0:T(8,128)(2,1)} %refs_3_.15, ...), custom_call_target="tpu_custom_call" | custom-call | flops 536870912 | bytes 4194304 | tf_op jit(solution)/shard_map/pallas_call | solution.py:333
  182.6 2.1 %collective-permute-start.21 = (bf16[128,2048]{1,0:T(8,128)(2,1)S(1)}, bf16[128,2048]{1,0:T(8,128)(2,1)S(1)}, u32[]{:S(2)}, u32[]{:S(2)}) collective-permute-start(bf16[128,2048]{1,0:T(8,128)(2,1)S(1)} %get-tuple-element.114), channel_id=1, source_target_pairs={{2,0},{4,2},{6,4},{7,6},{5,7},{3,5},{1,3},{0,1},{10,8},{12,10},{14... | collective-permute-start | bytes 1572872 | tf_op jit(solution)/shard_map/ppermute | solution.py:422
  184.7 6.2 %shard_map.116 = bf16[128,4096]{1,0:T(8,128)(2,1)S(1)} custom-call(s32[1]{0:T(128)} %bitcast.refs_0_, bf16[1024,512]{1,0:T(8,128)(2,1)S(1)} %get-tuple-element.100.refs_1_.refs_2_, bf16[512,4096]{1,0:T(8,128)(2,1)} %refs_3_.15), custom_call_target="tpu_custom_call" | custom-call | flops 536870912 | bytes 4194304 | tf_op jit(solution)/shard_map/pallas_call | solution.py:333
  191.1 3.2 %collective-permute-done.20 = bf16[128,2048]{1,0:T(8,128)(2,1)S(1)} collective-permute-done((bf16[128,2048]{1,0:T(8,128)(2,1)S(1)}, bf16[128,2048]{1,0:T(8,128)(2,1)S(1)}, u32[]{:S(2)}, u32[]{:S(2)}) %collective-permute-start.20) | collective-permute-done | bytes 524320 | tf_op jit(solution)/shard_map/ppermute | solution.py:419
  194.4 1.4 fusion.2
  (77 shorter events, 8.8 us)
Async XLA Ops:
  0.0 9.3 %slice-start = ((bf16[4096,256]{1,0:T(8,128)(2,1)}), bf16[4096,128]{1,0:T(8,128)(2,1)S(1)}, s32[]{:S(2)}) async-start(bf16[4096,256]{1,0:T(8,128)(2,1)} %refs_8_.1), calls=%async_computation | async-start | bytes 2097152 | tf_op jit(solution)/shard_map/slice | solution.py:373
  0.0 26.3 %collective-permute-start = (bf16[128,4096]{1,0:T(8,128)(2,1)}, bf16[128,4096]{1,0:T(8,128)(2,1)S(1)}, u32[]{:S(2)}, u32[]{:S(2)}) collective-permute-start(bf16[128,4096]{1,0:T(8,128)(2,1)} %refs_2_.2), channel_id=1, source_target_pairs={{0,2},{2,4},{4,6},{6,7},{7,5},{5,3},{3,1},{1,0},{8,10},{10,12},{12... | collective-permute-start | bytes 3145736 | tf_op jit(solution)/shard_map/ppermute | solution.py:419
  3.0 24.9 %collective-permute-start.1 = (bf16[128,4096]{1,0:T(8,128)(2,1)}, bf16[128,4096]{1,0:T(8,128)(2,1)}, u32[]{:S(2)}, u32[]{:S(2)}) collective-permute-start(bf16[128,4096]{1,0:T(8,128)(2,1)} %refs_2_.2), channel_id=1, source_target_pairs={{2,0},{4,2},{6,4},{7,6},{5,7},{3,5},{1,3},{0,1},{10,8},{12,10},{14... | collective-permute-start | bytes 3145736 | tf_op jit(solution)/shard_map/ppermute | solution.py:422
  11.1 3.3 %copy-start.4 = (bf16[4096]{0:T(1024)(128)(2,1)S(1)}, bf16[4096]{0:T(1024)(128)(2,1)}, u32[]{:S(2)}) copy-start(bf16[4096]{0:T(1024)(128)(2,1)} %param.12) | copy-start | bytes 24580
  11.1 3.3 %copy-start.3 = (s32[1024]{0:T(1024)S(1)}, s32[1024]{0:T(1024)}, u32[]{:S(2)}) copy-start(s32[1024]{0:T(1024)} %param.17) | copy-start | bytes 12292
  11.2 6.3 %copy-start = (bf16[128,4096]{1,0:T(8,128)(2,1)S(1)}, bf16[128,4096]{1,0:T(8,128)(2,1)}, u32[]{:S(2)}) copy-start(bf16[128,4096]{1,0:T(8,128)(2,1)} %refs_2_.2) | copy-start | bytes 3145732
  28.0 23.7 %collective-permute-start.2 = (bf16[128,4096]{1,0:T(8,128)(2,1)S(1)}, bf16[128,4096]{1,0:T(8,128)(2,1)S(1)}, u32[]{:S(2)}, u32[]{:S(2)}) collective-permute-start(bf16[128,4096]{1,0:T(8,128)(2,1)S(1)} %collective-permute-done.refs_2_), channel_id=1, source_target_pairs={{0,2},{2,4},{4,6},{6,7},{7,5},{5,3},{3,1},{1,0},{8,10},{10,12},{12... | collective-permute-start | bytes 3145736 | tf_op jit(solution)/shard_map/ppermute | solution.py:419
  29.5 23.6 %collective-permute-start.3 = (bf16[128,4096]{1,0:T(8,128)(2,1)}, bf16[128,4096]{1,0:T(8,128)(2,1)S(1)}, u32[]{:S(2)}, u32[]{:S(2)}) collective-permute-start(bf16[128,4096]{1,0:T(8,128)(2,1)} %collective-permute-done.1.refs_3_), channel_id=1, source_target_pairs={{2,0},{4,2},{6,4},{7,6},{5,7},{3,5},{1,3},{0,1},{10,8},{12,10},{14... | collective-permute-start | bytes 3145736 | tf_op jit(solution)/shard_map/ppermute | solution.py:422
  53.2 2.0 %copy-start.2 = (bf16[128,4096]{1,0:T(8,128)(2,1)}, bf16[128,4096]{1,0:T(8,128)(2,1)S(1)}, u32[]{:S(2)}) copy-start(bf16[128,4096]{1,0:T(8,128)(2,1)S(1)} %collective-permute-done.3.refs_3_) | copy-start | bytes 3145732
  53.2 22.5 %collective-permute-start.4 = (bf16[128,4096]{1,0:T(8,128)(2,1)S(1)}, bf16[128,4096]{1,0:T(8,128)(2,1)S(1)}, u32[]{:S(2)}, u32[]{:S(2)}) collective-permute-start(bf16[128,4096]{1,0:T(8,128)(2,1)S(1)} %collective-permute-done.2.refs_2_), channel_id=1, source_target_pairs={{0,2},{2,4},{4,6},{6,7},{7,5},{5,3},{3,1},{1,0},{8,10},{10,12},{12... | collective-permute-start | bytes 3145736 | tf_op jit(solution)/shard_map/ppermute | solution.py:419
  54.8 22.2 %collective-permute-start.5 = (bf16[128,4096]{1,0:T(8,128)(2,1)S(1)}, bf16[128,4096]{1,0:T(8,128)(2,1)S(1)}, u32[]{:S(2)}, u32[]{:S(2)}) collective-permute-start(bf16[128,4096]{1,0:T(8,128)(2,1)S(1)} %collective-permute-done.3.refs_3_), channel_id=1, source_target_pairs={{2,0},{4,2},{6,4},{7,6},{5,7},{3,5},{1,3},{0,1},{10,8},{12,10},{14... | collective-permute-start | bytes 3145736 | tf_op jit(solution)/shard_map/ppermute | solution.py:422
  77.0 4.2 %copy-start.1 = (bf16[128,4096]{1,0:T(8,128)(2,1)}, bf16[128,4096]{1,0:T(8,128)(2,1)S(1)}, u32[]{:S(2)}) copy-start(bf16[128,4096]{1,0:T(8,128)(2,1)S(1)} %collective-permute-done.5.refs_3_) | copy-start | bytes 3145732
  77.0 22.9 %collective-permute-start.6 = (bf16[64,4096]{1,0:T(8,128)(2,1)S(1)}, bf16[64,4096]{1,0:T(8,128)(2,1)S(1)}, u32[]{:S(2)}, u32[]{:S(2)}) collective-permute-start(bf16[64,4096]{1,0:T(8,128)(2,1)S(1)} %slice.146), channel_id=1, source_target_pairs={{0,2},{2,4},{4,6},{6,7},{7,5},{5,3},{3,1},{1,0},{8,10},{10,12},{12... | collective-permute-start | bytes 1572872 | tf_op jit(solution)/shard_map/ppermute | solution.py:419
  78.9 21.0 %collective-permute-start.7 = (bf16[64,4096]{1,0:T(8,128)(2,1)S(1)}, bf16[64,4096]{1,0:T(8,128)(2,1)S(1)}, u32[]{:S(2)}, u32[]{:S(2)}) collective-permute-start(bf16[64,4096]{1,0:T(8,128)(2,1)S(1)} %slice.147), channel_id=1, source_target_pairs={{2,0},{4,2},{6,4},{7,6},{5,7},{3,5},{1,3},{0,1},{10,8},{12,10},{14... | collective-permute-start | bytes 1572872 | tf_op jit(solution)/shard_map/ppermute | solution.py:422
  113.6 9.4 %collective-permute-start.8 = (bf16[128,2048]{1,0:T(8,128)(2,1)S(1)}, bf16[128,2048]{1,0:T(8,128)(2,1)S(1)}, u32[]{:S(2)}, u32[]{:S(2)}) collective-permute-start(bf16[128,2048]{1,0:T(8,128)(2,1)S(1)} %get-tuple-element.101), channel_id=1, source_target_pairs={{0,2},{2,4},{4,6},{6,7},{7,5},{5,3},{3,1},{1,0},{8,10},{10,12},{12... | collective-permute-start | bytes 1572872 | tf_op jit(solution)/shard_map/ppermute | solution.py:419
  115.7 14.6 %collective-permute-start.15 = (bf16[128,2048]{1,0:T(8,128)(2,1)S(1)}, bf16[128,2048]{1,0:T(8,128)(2,1)S(1)}, u32[]{:S(2)}, u32[]{:S(2)}) collective-permute-start(bf16[128,2048]{1,0:T(8,128)(2,1)S(1)} %get-tuple-element.108), channel_id=1, source_target_pairs={{2,0},{4,2},{6,4},{7,6},{5,7},{3,5},{1,3},{0,1},{10,8},{12,10},{14... | collective-permute-start | bytes 1572872 | tf_op jit(solution)/shard_map/ppermute | solution.py:422
  126.7 15.9 %collective-permute-start.10 = (bf16[128,2048]{1,0:T(8,128)(2,1)S(1)}, bf16[128,2048]{1,0:T(8,128)(2,1)S(1)}, u32[]{:S(2)}, u32[]{:S(2)}) collective-permute-start(bf16[128,2048]{1,0:T(8,128)(2,1)S(1)} %get-tuple-element.103), channel_id=1, source_target_pairs={{2,0},{4,2},{6,4},{7,6},{5,7},{3,5},{1,3},{0,1},{10,8},{12,10},{14... | collective-permute-start | bytes 1572872 | tf_op jit(solution)/shard_map/ppermute | solution.py:422
  130.2 14.9 %collective-permute-start.9 = (bf16[128,2048]{1,0:T(8,128)(2,1)S(1)}, bf16[128,2048]{1,0:T(8,128)(2,1)S(1)}, u32[]{:S(2)}, u32[]{:S(2)}) collective-permute-start(bf16[128,2048]{1,0:T(8,128)(2,1)S(1)} %get-tuple-element.102), channel_id=1, source_target_pairs={{0,2},{2,4},{4,6},{6,7},{7,5},{5,3},{3,1},{1,0},{8,10},{10,12},{12... | collective-permute-start | bytes 1572872 | tf_op jit(solution)/shard_map/ppermute | solution.py:419
  134.0 22.4 %collective-permute-start.16 = (bf16[128,2048]{1,0:T(8,128)(2,1)S(1)}, bf16[128,2048]{1,0:T(8,128)(2,1)S(1)}, u32[]{:S(2)}, u32[]{:S(2)}) collective-permute-start(bf16[128,2048]{1,0:T(8,128)(2,1)S(1)} %get-tuple-element.109), channel_id=1, source_target_pairs={{0,2},{2,4},{4,6},{6,7},{7,5},{5,3},{3,1},{1,0},{8,10},{10,12},{12... | collective-permute-start | bytes 1572872 | tf_op jit(solution)/shard_map/ppermute | solution.py:419
  136.1 20.3 %collective-permute-start.17 = (bf16[128,2048]{1,0:T(8,128)(2,1)S(1)}, bf16[128,2048]{1,0:T(8,128)(2,1)S(1)}, u32[]{:S(2)}, u32[]{:S(2)}) collective-permute-start(bf16[128,2048]{1,0:T(8,128)(2,1)S(1)} %get-tuple-element.110), channel_id=1, source_target_pairs={{2,0},{4,2},{6,4},{7,6},{5,7},{3,5},{1,3},{0,1},{10,8},{12,10},{14... | collective-permute-start | bytes 1572872 | tf_op jit(solution)/shard_map/ppermute | solution.py:422
  148.8 18.7 %collective-permute-start.11 = (bf16[128,2048]{1,0:T(8,128)(2,1)S(1)}, bf16[128,2048]{1,0:T(8,128)(2,1)S(1)}, u32[]{:S(2)}, u32[]{:S(2)}) collective-permute-start(bf16[128,2048]{1,0:T(8,128)(2,1)S(1)} %get-tuple-element.104), channel_id=1, source_target_pairs={{0,2},{2,4},{4,6},{6,7},{7,5},{5,3},{3,1},{1,0},{8,10},{10,12},{12... | collective-permute-start | bytes 1572872 | tf_op jit(solution)/shard_map/ppermute | solution.py:419
  148.9 18.7 %collective-permute-start.12 = (bf16[128,2048]{1,0:T(8,128)(2,1)S(1)}, bf16[128,2048]{1,0:T(8,128)(2,1)S(1)}, u32[]{:S(2)}, u32[]{:S(2)}) collective-permute-start(bf16[128,2048]{1,0:T(8,128)(2,1)S(1)} %get-tuple-element.105), channel_id=1, source_target_pairs={{2,0},{4,2},{6,4},{7,6},{5,7},{3,5},{1,3},{0,1},{10,8},{12,10},{14... | collective-permute-start | bytes 1572872 | tf_op jit(solution)/shard_map/ppermute | solution.py:422
  160.1 18.7 %collective-permute-start.18 = (bf16[128,2048]{1,0:T(8,128)(2,1)S(1)}, bf16[128,2048]{1,0:T(8,128)(2,1)S(1)}, u32[]{:S(2)}, u32[]{:S(2)}) collective-permute-start(bf16[128,2048]{1,0:T(8,128)(2,1)S(1)} %get-tuple-element.111), channel_id=1, source_target_pairs={{0,2},{2,4},{4,6},{6,7},{7,5},{5,3},{3,1},{1,0},{8,10},{10,12},{12... | collective-permute-start | bytes 1572872 | tf_op jit(solution)/shard_map/ppermute | solution.py:419
  160.1 18.7 %collective-permute-start.19 = (bf16[128,2048]{1,0:T(8,128)(2,1)S(1)}, bf16[128,2048]{1,0:T(8,128)(2,1)S(1)}, u32[]{:S(2)}, u32[]{:S(2)}) collective-permute-start(bf16[128,2048]{1,0:T(8,128)(2,1)S(1)} %get-tuple-element.112), channel_id=1, source_target_pairs={{2,0},{4,2},{6,4},{7,6},{5,7},{3,5},{1,3},{0,1},{10,8},{12,10},{14... | collective-permute-start | bytes 1572872 | tf_op jit(solution)/shard_map/ppermute | solution.py:422
  171.3 19.7 %collective-permute-start.13 = (bf16[128,2048]{1,0:T(8,128)(2,1)S(1)}, bf16[128,2048]{1,0:T(8,128)(2,1)S(1)}, u32[]{:S(2)}, u32[]{:S(2)}) collective-permute-start(bf16[128,2048]{1,0:T(8,128)(2,1)S(1)} %get-tuple-element.106), channel_id=1, source_target_pairs={{0,2},{2,4},{4,6},{6,7},{7,5},{5,3},{3,1},{1,0},{8,10},{10,12},{12... | collective-permute-start | bytes 1572872 | tf_op jit(solution)/shard_map/ppermute | solution.py:419
  171.3 19.6 %collective-permute-start.14 = (bf16[128,2048]{1,0:T(8,128)(2,1)S(1)}, bf16[128,2048]{1,0:T(8,128)(2,1)S(1)}, u32[]{:S(2)}, u32[]{:S(2)}) collective-permute-start(bf16[128,2048]{1,0:T(8,128)(2,1)S(1)} %get-tuple-element.107), channel_id=1, source_target_pairs={{2,0},{4,2},{6,4},{7,6},{5,7},{3,5},{1,3},{0,1},{10,8},{12,10},{14... | collective-permute-start | bytes 1572872 | tf_op jit(solution)/shard_map/ppermute | solution.py:422
  182.5 11.7 %collective-permute-start.20 = (bf16[128,2048]{1,0:T(8,128)(2,1)S(1)}, bf16[128,2048]{1,0:T(8,128)(2,1)S(1)}, u32[]{:S(2)}, u32[]{:S(2)}) collective-permute-start(bf16[128,2048]{1,0:T(8,128)(2,1)S(1)} %get-tuple-element.113), channel_id=1, source_target_pairs={{0,2},{2,4},{4,6},{6,7},{7,5},{5,3},{3,1},{1,0},{8,10},{10,12},{12... | collective-permute-start | bytes 1572872 | tf_op jit(solution)/shard_map/ppermute | solution.py:419
  182.6 11.7 %collective-permute-start.21 = (bf16[128,2048]{1,0:T(8,128)(2,1)S(1)}, bf16[128,2048]{1,0:T(8,128)(2,1)S(1)}, u32[]{:S(2)}, u32[]{:S(2)}) collective-permute-start(bf16[128,2048]{1,0:T(8,128)(2,1)S(1)} %get-tuple-element.114), channel_id=1, source_target_pairs={{2,0},{4,2},{6,4},{7,6},{5,7},{3,5},{1,3},{0,1},{10,8},{12,10},{14... | collective-permute-start | bytes 1572872 | tf_op jit(solution)/shard_map/ppermute | solution.py:422
where the time goes:
time: 197 us; the launch traced here: 196 us
  Pallas kernels  108 us (55%)
  waiting for transfers between devices  39.9 us (20%)
  starting transfers between devices  25.5 us (13%)
  other arithmetic  16.6 us (8%)
  local copies, waits for them, and re-layouts  5.62 us (3%)
    pallas_call x6, Pallas kernels, run_step(): pl.pallas_call(functools.partial(step_kernel, pieces, rows, heads), grid_...  75.3 us
    pallas_call x8, Pallas kernels, run_send(): pl.pallas_call(functools.partial(send_kernel, [len(group) for group in ar...  32.7 us
    ppermute x11, waiting for transfers between devices, forward(): return lax.ppermute(x, 'tensor', forward_pairs)  30.3 us
    ppermute x11, starting transfers between devices, backward(): return lax.ppermute(x, 'tensor', backward_pairs)  13 us
    ppermute x11, starting transfers between devices, forward(): return lax.ppermute(x, 'tensor', forward_pairs)  12.4 us
    ppermute x11, waiting for transfers between devices, backward(): return lax.ppermute(x, 'tensor', backward_pairs)  9.53 us
    another operation x4, other arithmetic, ids_of(): return jnp.stack([my_around[d % size] for d in distances])  4.81 us
  transfers between devices with their start and end apart: 22, of which 12 were waited for; matrix products, arithmetic and copies ran while one was open for 11% of the time, Pallas kernels for 48%

commit v1 on v0

--- a/solution.py
+++ b/solution.py
@@ -32,25 +32,34 @@
     return [z * ys + y for z, y in cycle]
 
 
+def arrival_slots(order, rank):
+    size = len(order)
+    half = size // 2
+    place = {r: i for i, r in enumerate(order)}
+    slots = {}
+    for chunk in range(size):
+        behind = (place[rank] - place[chunk]) % size
+        if behind == 0:
+            slots[chunk, 0] = slots[chunk, 1] = 0
+        elif behind < half:
+            slots[chunk, 0], slots[chunk, 1] = 2 * behind - 1, 2 * behind
+        elif behind == half:
+            slots[chunk, 0] = slots[chunk, 1] = size - 1
+        else:
+            slots[chunk, 1], slots[chunk, 0] = 2 * (size - behind) - 1, 2 * (size - behind)
+    return slots
+
+
 def ready_tiles(order):
     size = len(order)
-    place = {rank: i for i, rank in enumerate(order)}
-
-    def distance(a, b):
-        apart = (place[a] - place[b]) % size
-        return min(apart, size - apart)
-
-    steps = size // 2 + 1
-    found = [[[] for _ in range(steps + 1)] for _ in range(size)]
+    found = [[[] for _ in range(size)] for _ in range(size)]
     for rank in range(size):
-        last = order[(place[rank] + size // 2) % size]
+        slots = arrival_slots(order, rank)
         for chunk in range(size):
-            own = distance(rank, chunk)
-            before = distance(rank, chunk - 1) if chunk else 0
-            late = steps if max(own, before) == size // 2 and chunk != last else None
-            first = max(own, before)
-            found[rank][first if late is None else late].append(2 * chunk)
-            found[rank][own].append(2 * chunk + 1)
+            before = slots[chunk - 1, 1] if chunk else slots[chunk, 1]
+            lower = max(slots[chunk, 0], before)
+            found[rank][lower].append(2 * chunk)
+            found[rank][max(slots[chunk, 0], slots[chunk, 1])].append(2 * chunk + 1)
     return found
 
 
@@ -284,7 +293,6 @@
         pltpu.SemaphoreType.DMA((2, 4)),
         pltpu.SemaphoreType.DMA,
     ]
-    flops = 2 * pieces * rows * depth * (width + 256) + 2 * 2 * 2 * TILE * width * prefix
     return pl.pallas_call(
         functools.partial(step_kernel, pieces, rows, heads),
         grid_spec=pltpu.PrefetchScalarGridSpec(
@@ -297,50 +305,43 @@
         out_shape=out_shape,
         input_output_aliases=aliases,
         compiler_params=pltpu.CompilerParams(vmem_limit_bytes=VMEM_LIMIT),
-        cost_estimate=pl.CostEstimate(flops=flops, bytes_accessed=12 << 20, transcendentals=0),
+        cost_estimate=pl.CostEstimate(flops=1 << 20, bytes_accessed=1 << 16, transcendentals=0),
     )(ids, lists, *operands)
 
 
-def send_kernel(has, shared, *refs):
-    count = len(has)
+def send_kernel(added, *refs):
     rest = iter(refs[1:])
-    atts = [next(rest) for _ in range(count)]
-    weights = [next(rest)] * count if shared else [next(rest) for _ in range(count)]
-    arrived = [[next(rest) for _ in range(many)] for many in has]
-    outs = refs[-count:]
-    for i in range(count):
-        made = jnp.dot(atts[i][...], weights[i][...], preferred_element_type=jnp.float32)
-        made = made.astype(jnp.bfloat16).astype(jnp.float32)
-        for other in arrived[i]:
-            made = made + other[...].astype(jnp.float32)
-        outs[i][...] = made.astype(jnp.bfloat16)
-
-
-def run_send(ids, att, w_out, arrived, pieces, chunk_rows, columns):
-    count = len(arrived)
-    block = 512
-    per_piece = columns // block
-    width = att.shape[1]
-    shared = len(set(pieces)) == 1
-    used = pieces[:1] if shared else pieces
-    row_block = pl.BlockSpec((chunk_rows, block), lambda b, ids: (0, b))
-    in_specs = [pl.BlockSpec((chunk_rows, width), lambda b, ids, i=i: (ids[i], 0)) for i in range(count)]
-    in_specs += [pl.BlockSpec((width, block), lambda b, ids, p=p: (0, p * per_piece + b)) for p in used]
-    operands = [att] * count + [w_out] * len(used)
-    for group in arrived:
-        operands += group
-        in_specs += [row_block] * len(group)
+    first, second, weights = next(rest), next(rest), next(rest)
+    arrived = [next(rest) if has else None for has in added]
+    outs = refs[-2:]
+    both = jnp.concatenate([first[...], second[...]], axis=0)
+    made = jnp.dot(both, weights[...], preferred_element_type=jnp.float32).astype(jnp.bfloat16)
+    for i in range(2):
+        mine = made[i * TILE:(i + 1) * TILE]
+        if arrived[i] is not None:
+            mine = (mine.astype(jnp.float32) + arrived[i][...].astype(jnp.float32)).astype(jnp.bfloat16)
+        outs[i][...] = mine
+
+
+def run_send(ids, att, w_out, arrived=(None, None)):
+    width, columns = w_out.shape
+    block = 1024
+    row_block = pl.BlockSpec((TILE, block), lambda b, ids: (0, b))
+    in_specs = [pl.BlockSpec((TILE, width), lambda b, ids, i=i: (ids[i], 0)) for i in range(2)]
+    in_specs.append(pl.BlockSpec((width, block), lambda b, ids: (0, b)))
+    given = [other for other in arrived if other is not None]
     return pl.pallas_call(
-        functools.partial(send_kernel, [len(group) for group in arrived], shared),
+        functools.partial(send_kernel, [other is not None for other in arrived]),
         grid_spec=pltpu.PrefetchScalarGridSpec(
-            num_scalar_prefetch=1, grid=(per_piece,), in_specs=in_specs, out_specs=[row_block] * count
+            num_scalar_prefetch=1,
+            grid=(columns // block,),
+            in_specs=in_specs + [row_block] * len(given),
+            out_specs=[row_block] * 2,
         ),
-        out_shape=[jax.ShapeDtypeStruct((chunk_rows, columns), jnp.bfloat16)] * count,
+        out_shape=[jax.ShapeDtypeStruct((TILE, columns), jnp.bfloat16)] * 2,
         compiler_params=pltpu.CompilerParams(vmem_limit_bytes=VMEM_LIMIT),
-        cost_estimate=pl.CostEstimate(
-            flops=2 * count * chunk_rows * width * columns, bytes_accessed=4 << 20, transcendentals=0
-        ),
-    )(ids, *operands)
+        cost_estimate=pl.CostEstimate(flops=1 << 20, bytes_accessed=1 << 16, transcendentals=0),
+    )(ids, att, att, w_out, *given)
 
 
 def tables(seg_ids, seg_doc, doc_lens, prefix, cache):
@@ -437,21 +438,28 @@
         )
 
     place = {r: i for i, r in enumerate(order)}
-    around = np.array([[order[(place[r] + d) % size] for d in range(size)] for r in range(size)], np.int32)
     ready = ready_tiles(order)
-    most = max(len(ready[r][s]) for r in range(size) for s in range(half + 2))
-    plan = np.zeros((size, half + 2, 3 + most), np.int32)
+    most = max(len(tiles) for by_slot in ready for tiles in by_slot)
+    plan = np.zeros((size, size, 3 + most), np.int32)
+    sends = np.zeros((size, half + 1, 2, 2), np.int32)
+    flips = np.zeros((size,), np.int32)
     for r in range(size):
-        for s in range(half + 2):
-            ids = [0, 0]
-            if s < half:
-                ids = [2 * around[r][(-s) % size], 2 * around[r][s]]
-            elif s == half:
-                ids = [2 * around[r][half], 2 * around[r][half] + 1]
+        flips[r] = int(order[(place[r] - 1) % size] == r - 1)
+    for r in range(size):
+        for s in range(size):
+            d = (s + 1) // 2
+            back, ahead = 2 * order[(place[r] - d) % size], 2 * order[(place[r] + d) % size]
+            late = int(s % 2 == 0 and s > 0)
+            ids = [2 * r, 0] if s == 0 else [back + late, ahead + 1 - late]
             row = ids + [len(ready[r][s])] + ready[r][s]
             plan[r, s, :len(row)] = row
+        for d in range(half + 1):
+            ahead, back = order[(place[r] + d) % size], order[(place[r] - d) % size]
+            sends[r, d, 0] = [2 * ahead + flips[ahead], 2 * back + 1 - flips[back]]
+            sends[r, d, 1] = [2 * ahead + 1 - flips[ahead], 2 * back + flips[back]]
     my_plan = jnp.asarray(plan)[rank]
-    my_around = jnp.asarray(around)[rank]
+    my_sends = jnp.asarray(sends)[rank]
+    flipped = jnp.asarray(flips)[rank] > 0
 
     cosine, sine, key_wide, doc_bias, own_bias, lists = tables(
         seg_ids, seg_doc, doc_lens, prefix, prefix_keyvalue_cache
@@ -460,43 +468,45 @@
     fixed = (gain, w_query, keyvalue_weight, cosine, sine, key_wide, prefix_keyvalue_cache, doc_bias, own_bias)
     dims = (tokens, heads, prefix, depth)
 
-    from_left, from_right = hidden_in, hidden_in
-    state = None
-    held = [hidden_in]
-    for s in range(half):
-        if s + 1 < half:
-            next_left, next_right = forward(from_left), backward(from_right)
+    lower, upper = hidden_in[:TILE], hidden_in[TILE:]
+    pieces = {1: (forward(lower), backward(upper)), 2: (forward(upper), backward(lower))}
+    state = run_step(my_plan[0], lists, [hidden_in], fixed, None, dims)
+    for slot in range(1, size - 1):
+        pieces[slot], state = lax.optimization_barrier((pieces[slot], tuple(state)))
+        if slot < size - 2:
+            following = min(slot + 2, size - 1)
+            pieces[following] = (forward(pieces[slot][0]), backward(pieces[slot][1]))
+        state = run_step(my_plan[slot], lists, pieces[slot], fixed, state, dims)
+
+    def send(distance, stream, att, arrived=(None, None)):
+        made = run_send(my_sends[distance, stream], att, w_out, arrived)
+        return (made[0], made[1])
+
+    early = send(half - 1, 1, state[2])
+    early, pieces[size - 1], state = lax.optimization_barrier((early, pieces[size - 1], tuple(state)))
+    early = (forward(early[0]), backward(early[1]))
+    state = run_step(my_plan[size - 1], lists, pieces[size - 1], fixed, state, dims)
+    early, state = lax.optimization_barrier((early, tuple(state)))
+    made = send(half, 0, state[2])
+    far = (forward(made[0]), backward(made[1]))
+    early, made = lax.optimization_barrier((early, made))
+    att = state[2]
+    for distance in range(half - 1, 0, -1):
+        if distance > 1:
+            made = send(distance - 1, 1, att, early)
+            early = (forward(made[0]), backward(made[1]))
+            far, made = lax.optimization_barrier((far, made))
         else:
-            next_left, next_right = forward(from_left[:TILE]), backward(from_right[TILE:])
-        state = run_step(my_plan[s], lists, held, fixed, state, dims)
-        (next_left, next_right), state = lax.optimization_barrier(((next_left, next_right), tuple(state)))
-        from_left, from_right = next_left, next_right
-        held = [from_left, from_right]
-    state = run_step(my_plan[half], lists, held, fixed, state, dims)
-    columns = depth // 2
-
-    def ids_of(*distances):
-        return jnp.stack([my_around[d % size] for d in distances])
-
-    sent = run_send(ids_of(half, half), state[2], w_out, [[], []], [0, 1], chunk_rows, columns)
-    sent, state = lax.optimization_barrier((tuple(sent), tuple(state)))
-    arrived = [[[forward(sent[0])], []], [[], [backward(sent[1])]]]
-    att = run_step(my_plan[half + 1], lists, [], fixed, state, dims)[2]
-    for d in range(half - 1, 0, -1):
-        following = []
-        for piece in range(2):
-            made = run_send(ids_of(d, -d), att, w_out, arrived[piece], [piece, piece], chunk_rows, columns)
-            following.append([[forward(made[0])], [backward(made[1])]])
-        arrived = following
-    own = run_send(ids_of(0), att, w_out, [[]], [0], chunk_rows, depth)[0]
-    result = hidden_in.astype(jnp.float32) + own.astype(jnp.float32)
-    (left_0,), (right_0,) = arrived[0]
-    (left_1,), (right_1,) = arrived[1]
-    summed = jnp.concatenate(
-        [left.astype(jnp.float32) + right.astype(jnp.float32) for left, right in ((left_0, right_0), (left_1, right_1))],
-        axis=1,
-    )
-    return (result + summed).astype(jnp.bfloat16)
+            early, far = lax.optimization_barrier((early, far))
+        made = send(distance, 0, att, far)
+        far = (forward(made[0]), backward(made[1]))
+        early, made = lax.optimization_barrier((early, made))
+    own = run_send(jnp.stack([2 * rank, 2 * rank + 1]).astype(jnp.int32), att, w_out)
+    wide = [[part.astype(jnp.float32) for part in pair] for pair in (early, far)]
+    with_far, with_early = wide[1][0] + wide[0][1], wide[0][0] + wide[1][1]
+    halves = [jnp.where(flipped, with_early, with_far), jnp.where(flipped, with_far, with_early)]
+    summed = jnp.concatenate([halves[i] + own[i].astype(jnp.float32) for i in range(2)], axis=0)
+    return (hidden_in.astype(jnp.float32) + summed).astype(jnp.bfloat16)
 
 
 def solution(mesh):

time: 197 us -> 205 us (1.041)
  starting transfers between devices: 25.5 us -> 33.8 us
  other arithmetic: 16.6 us -> 13.8 us
  local copies, waits for them, and re-layouts: 5.62 us -> 8.13 us
    ppermute x11 -> x14, waiting for transfers between devices: 9.53 us -> 17.1 us  [backward(): return lax.ppermute(x, 'tensor', backward_pairs)]
    ppermute x11 -> x14, waiting for transfers between devices: 30.3 us -> 23.8 us  [forward(): return lax.ppermute(x, 'tensor', forward_pairs)]
    another operation x4 -> x1, other arithmetic: 4.81 us -> 0.08 us  [local(): jnp.stack([2 * rank, 2 * rank + 1]).astype(jnp.int32)]
    ppermute x11 -> x14, starting transfers between devices: 12.4 us -> 16.8 us  [forward(): return lax.ppermute(x, 'tensor', forward_pairs)]
    ppermute x11 -> x14, starting transfers between devices: 13 us -> 17.1 us  [backward(): return lax.ppermute(x, 'tensor', backward_pairs)]
    pallas_call x6 -> x8, Pallas kernels: 75.3 us -> 73.5 us  [run_step(): pl.pallas_call(functools.partial(step_kernel, pieces, rows, heads), grid_...]
  transfers between devices with their start and end apart: 22 -> 28, of which waited for: 12 -> 13; matrix products, arithmetic and copies ran while one was open for 11% -> 8% of each run, Pallas kernels for 48% -> 48%
where the time goes in v1:
time: 205 us; the launch traced here: 204 us
  Pallas kernels  106 us (52%)
  waiting for transfers between devices  40.9 us (20%)
  starting transfers between devices  33.8 us (16%)
  other arithmetic  13.8 us (7%)
  local copies, waits for them, and re-layouts  8.13 us (4%)
    pallas_call x8, Pallas kernels, run_step(): pl.pallas_call(functools.partial(step_kernel, pieces, rows, heads), grid_...  73.5 us
    pallas_call x8, Pallas kernels, run_send(): pl.pallas_call(functools.partial(send_kernel, [other is not None for othe...  33 us
    ppermute x14, waiting for transfers between devices, forward(): return lax.ppermute(x, 'tensor', forward_pairs)  23.8 us
    ppermute x14, starting transfers between devices, backward(): return lax.ppermute(x, 'tensor', backward_pairs)  17.1 us
    ppermute x14, waiting for transfers between devices, backward(): return lax.ppermute(x, 'tensor', backward_pairs)  17.1 us
    ppermute x14, starting transfers between devices, forward(): return lax.ppermute(x, 'tensor', forward_pairs)  16.8 us
  transfers between devices with their start and end apart: 28, of which 13 were waited for; matrix products, arithmetic and copies ran while one was open for 8% of the time, Pallas kernels for 48%

profile of v1, /device:TPU:0, one launch (start us, length us, event | category | flops | bytes accessed | tf_op | source)
XLA Modules:
  0.0 204.2 jit_solution(8540435214254939807)
XLA Ops:
  0.0 2.4 %fusion.11 = (bf16[64,4096]{1,0:T(8,128)(2,1)}, bf16[64,4096]{1,0:T(8,128)(2,1)}) fusion(bf16[128,4096]{1,0:T(8,128)(2,1)} %refs_2_.1), kind=kLoop, calls=%fused_computation.77 | loop fusion | bytes 2097152 | tf_op jit(solution)/shard_map/slice | solution.py:471
  2.4 3.0 %collective-permute-start.3 = (bf16[64,4096]{1,0:T(8,128)(2,1)}, bf16[64,4096]{1,0:T(8,128)(2,1)}, u32[]{:S(2)}, u32[]{:S(2)}) collective-permute-start(bf16[64,4096]{1,0:T(8,128)(2,1)} %get-tuple-element.203), channel_id=1, source_target_pairs={{2,0},{4,2},{6,4},{7,6},{5,7},{3,5},{1,3},{0,1},{10,8},{12,10},{14... | collective-permute-start | bytes 1572872 | tf_op jit(solution)/shard_map/ppermute | solution.py:423
  5.4 2.0 collective-permute-start.2
  12.1 1.3 convert_reduce_fusion
  15.0 1.3 copy.41
  16.9 2.9 %fusion.1.refs_8_.refs_9_ = bf16[17,256,256]{2,1,0:T(8,128)(2,1)} fusion(bf16[16,128,256]{2,1,0:T(8,128)(2,1)} %bitcast.49, bf16[17,128,256]{2,1,0:T(8,128)(2,1)S(1)} %and_convert_fusion), kind=kLoop, calls=%fused_computation.3 | loop fusion | flops 6684672 | bytes 4390912 | tf_op jit(solution)/shard_map/concatenate | solution.py:375
  20.3 1.9 fusion.3
  22.6 8.8 %shard_map.118 = (bf16[4,1024,128]{2,1,0:T(8,128)(2,1)S(1)}, bf16[1024,256]{1,0:T(8,128)(2,1)S(1)}, bf16[1024,512]{1,0:T(8,128)(2,1)S(1)}) custom-call(s32[7]{0:T(128)S(1)} %get-tuple-element.211.refs_0_, s32[320]{0:T(512)S(1)} %reshape.300.refs_1_, bf16[128,4096]{1,0:T(8,128)(2,1)S(1)} %copy-done, f32[1,4096]{1,0:T(1,128)S(1)} %bitcast.40, ...), custom_call_target="tpu_custom_call" | custom-call | flops 1048576 | bytes 65536 | tf_op jit(solution)/shard_map/pallas_call | solution.py:296
  31.5 2.0 collective-permute-start.7
  33.5 8.6 %shard_map.119 = (bf16[4,1024,128]{2,1,0:T(8,128)(2,1)S(1)}, bf16[1024,256]{1,0:T(8,128)(2,1)S(1)}, bf16[1024,512]{1,0:T(8,128)(2,1)S(1)}) custom-call(s32[7]{0:T(128)S(1)} %get-tuple-element.212.refs_0_, s32[320]{0:T(512)S(1)} %reshape.300.refs_1_, ...), custom_call_target="tpu_custom_call", output_to_operand_aliasing={{0}: (13, {}), {1}: (14, {}), {2}: (15, {})} | custom-call | flops 1048576 | bytes 65536 | tf_op jit(solution)/shard_map/pallas_call | solution.py:296
  42.2 2.0 collective-permute-start.5
  44.2 10.3 %shard_map.120 = (bf16[4,1024,128]{2,1,0:T(8,128)(2,1)S(1)}, bf16[1024,256]{1,0:T(8,128)(2,1)S(1)}, bf16[1024,512]{1,0:T(8,128)(2,1)S(1)}) custom-call(s32[7]{0:T(128)S(1)} %get-tuple-element.209.refs_0_, s32[320]{0:T(512)S(1)} %reshape.300.refs_1_, ...), custom_call_target="tpu_custom_call", output_to_operand_aliasing={{0}: (13, {}), {1}: (14, {}), {2}: (15, {})} | custom-call | flops 1048576 | bytes 65536 | tf_op jit(solution)/shard_map/pallas_call | solution.py:296
  56.6 6.8 %shard_map.121 = (bf16[4,1024,128]{2,1,0:T(8,128)(2,1)S(1)}, bf16[1024,256]{1,0:T(8,128)(2,1)S(1)}, bf16[1024,512]{1,0:T(8,128)(2,1)S(1)}) custom-call(s32[7]{0:T(128)S(1)} %get-tuple-element.210.refs_0_, s32[320]{0:T(512)S(1)} %reshape.300.refs_1_, ...), custom_call_target="tpu_custom_call", output_to_operand_aliasing={{0}: (13, {}), {1}: (14, {}), {2}: (15, {})} | custom-call | flops 1048576 | bytes 65536 | tf_op jit(solution)/shard_map/pallas_call | solution.py:296
  64.4 1.2 collective-permute-start.9
  65.5 11.5 %shard_map.122 = (bf16[4,1024,128]{2,1,0:T(8,128)(2,1)S(1)}, bf16[1024,256]{1,0:T(8,128)(2,1)S(1)}, bf16[1024,512]{1,0:T(8,128)(2,1)S(1)}) custom-call(s32[7]{0:T(128)S(1)} %get-tuple-element.207.refs_0_, s32[320]{0:T(512)S(1)} %reshape.300.refs_1_, ...), custom_call_target="tpu_custom_call", output_to_operand_aliasing={{0}: (13, {}), {1}: (14, {}), {2}: (15, {})} | custom-call | flops 1048576 | bytes 65536 | tf_op jit(solution)/shard_map/pallas_call | solution.py:296
  77.4 1.8 collective-permute-start.13
  80.2 6.4 %shard_map.123 = (bf16[4,1024,128]{2,1,0:T(8,128)(2,1)S(1)}, bf16[1024,256]{1,0:T(8,128)(2,1)S(1)}, bf16[1024,512]{1,0:T(8,128)(2,1)S(1)}) custom-call(s32[7]{0:T(128)S(1)} %get-tuple-element.208.refs_0_, s32[320]{0:T(512)S(1)} %reshape.300.refs_1_, ...), custom_call_target="tpu_custom_call", output_to_operand_aliasing={{0}: (13, {}), {1}: (14, {}), {2}: (15, {})} | custom-call | flops 1048576 | bytes 65536 | tf_op jit(solution)/shard_map/pallas_call | solution.py:296
  86.6 11.6 %shard_map.124 = (bf16[4,1024,128]{2,1,0:T(8,128)(2,1)S(1)}, bf16[1024,256]{1,0:T(8,128)(2,1)S(1)}, bf16[1024,512]{1,0:T(8,128)(2,1)S(1)}) custom-call(s32[7]{0:T(128)S(1)} %get-tuple-element.213.refs_0_, s32[320]{0:T(512)S(1)} %reshape.300.refs_1_, ...), custom_call_target="tpu_custom_call", output_to_operand_aliasing={{0}: (13, {}), {1}: (14, {}), {2}: (15, {})} | custom-call | flops 1048576 | bytes 65536 | tf_op jit(solution)/shard_map/pallas_call | solution.py:296
  98.1 4.1 %shard_map.125 = (bf16[64,4096]{1,0:T(8,128)(2,1)S(1)}, bf16[64,4096]{1,0:T(8,128)(2,1)S(1)}) custom-call(s32[2]{0:T(128)S(1)} %get-tuple-element.198.refs_0_, bf16[1024,512]{1,0:T(8,128)(2,1)S(1)} %get-tuple-element.158.refs_1_.refs_2_.refs_15_, bf16[1024,512]{1,0:T(8,128)(2,1)S(1)} %get-tuple-element.158.refs_1_.refs_2_.refs_15_, bf16[512,4096]{1,0:T(8,128)(2,1)} %refs_3_.15), custom_call_target="tpu_custom_call" | custom-call | flops 1048576 | bytes 65536 | tf_op jit(solution)/shard_map/pallas_call | solution.py:333
  102.3 5.9 %collective-permute-start.14 = (bf16[64,4096]{1,0:T(8,128)(2,1)S(1)}, bf16[64,4096]{1,0:T(8,128)(2,1)S(1)}, u32[]{:S(2)}, u32[]{:S(2)}) collective-permute-start(bf16[64,4096]{1,0:T(8,128)(2,1)S(1)} %get-tuple-element.152), channel_id=1, source_target_pairs={{0,2},{2,4},{4,6},{6,7},{7,5},{5,3},{3,1},{1,0},{8,10},{10,12},{12... | collective-permute-start | bytes 1572872 | tf_op jit(solution)/shard_map/ppermute | solution.py:420
  108.2 9.5 %shard_map.126 = (bf16[4,1024,128]{2,1,0:T(8,128)(2,1)S(1)}, bf16[1024,256]{1,0:T(8,128)(2,1)S(1)}, bf16[1024,512]{1,0:T(8,128)(2,1)S(1)}) custom-call(s32[7]{0:T(128)S(1)} %get-tuple-element.206.refs_0_, s32[320]{0:T(512)S(1)} %reshape.300.refs_1_, ...), custom_call_target="tpu_custom_call", output_to_operand_aliasing={{0}: (13, {}), {1}: (14, {}), {2}: (15, {})} | custom-call | flops 1048576 | bytes 65536 | tf_op jit(solution)/shard_map/pallas_call | solution.py:296
  117.7 4.1 %collective-permute-done.15.refs_5_ = bf16[64,4096]{1,0:T(8,128)(2,1)S(1)} collective-permute-done((bf16[64,4096]{1,0:T(8,128)(2,1)S(1)}, bf16[64,4096]{1,0:T(8,128)(2,1)S(1)}, u32[]{:S(2)}, u32[]{:S(2)}) %collective-permute-start.15) | collective-permute-done | bytes 524320 | tf_op jit(solution)/shard_map/ppermute | solution.py:423
  121.8 4.1 %shard_map.127 = (bf16[64,4096]{1,0:T(8,128)(2,1)S(1)}, bf16[64,4096]{1,0:T(8,128)(2,1)S(1)}) custom-call(s32[2]{0:T(128)S(1)} %get-tuple-element.196.refs_0_, bf16[1024,512]{1,0:T(8,128)(2,1)S(1)} %get-tuple-element.160.refs_1_.refs_2_, bf16[1024,512]{1,0:T(8,128)(2,1)S(1)} %get-tuple-element.160.refs_1_.refs_2_, bf16[512,4096]{1,0:T(8,128)(2,1)} %refs_3_.15), custom_call_target="tpu_custom_call" | custom-call | flops 1048576 | bytes 65536 | tf_op jit(solution)/shard_map/pallas_call | solution.py:333
  125.9 1.8 collective-permute-start.18
  128.0 4.1 %shard_map.128 = (bf16[64,4096]{1,0:T(8,128)(2,1)S(1)}, bf16[64,4096]{1,0:T(8,128)(2,1)S(1)}) custom-call(s32[2]{0:T(128)S(1)} %get-tuple-element.197.refs_0_, bf16[1024,512]{1,0:T(8,128)(2,1)S(1)} %get-tuple-element.160.refs_1_.refs_2_, bf16[1024,512]{1,0:T(8,128)(2,1)S(1)} %get-tuple-element.160.refs_1_.refs_2_, bf16[512,4096]{1,0:T(8,128)(2,1)} %refs_3_.15, ...), custom_call_target="tpu_custom_call" | custom-call | flops 1048576 | bytes 65536 | tf_op jit(solution)/shard_map/pallas_call | solution.py:333
  132.1 1.8 collective-permute-start.16
  134.2 6.6 %collective-permute-done.18.refs_4_ = bf16[64,4096]{1,0:T(8,128)(2,1)S(1)} collective-permute-done((bf16[64,4096]{1,0:T(8,128)(2,1)S(1)}, bf16[64,4096]{1,0:T(8,128)(2,1)S(1)}, u32[]{:S(2)}, u32[]{:S(2)}) %collective-permute-start.18) | collective-permute-done | bytes 524320 | tf_op jit(solution)/shard_map/ppermute | solution.py:420
  140.8 1.7 collective-permute-done.19.refs_5_
  142.5 4.1 %shard_map.129 = (bf16[64,4096]{1,0:T(8,128)(2,1)S(1)}, bf16[64,4096]{1,0:T(8,128)(2,1)S(1)}) custom-call(s32[2]{0:T(128)S(1)} %get-tuple-element.195.refs_0_, bf16[1024,512]{1,0:T(8,128)(2,1)S(1)} %get-tuple-element.160.refs_1_.refs_2_, bf16[1024,512]{1,0:T(8,128)(2,1)S(1)} %get-tuple-element.160.refs_1_.refs_2_, bf16[512,4096]{1,0:T(8,128)(2,1)} %refs_3_.15, ...), custom_call_target="tpu_custom_call" | custom-call | flops 1048576 | bytes 65536 | tf_op jit(solution)/shard_map/pallas_call | solution.py:333
  147.1 1.7 collective-permute-start.23
  148.8 3.3 %collective-permute-done.16.refs_4_ = bf16[64,4096]{1,0:T(8,128)(2,1)S(1)} collective-permute-done((bf16[64,4096]{1,0:T(8,128)(2,1)S(1)}, bf16[64,4096]{1,0:T(8,128)(2,1)S(1)}, u32[]{:S(2)}, u32[]{:S(2)}) %collective-permute-start.16) | collective-permute-done | bytes 524320 | tf_op jit(solution)/shard_map/ppermute | solution.py:420
  152.0 1.7 collective-permute-done.17.refs_5_
  153.8 4.1 %shard_map.130 = (bf16[64,4096]{1,0:T(8,128)(2,1)S(1)}, bf16[64,4096]{1,0:T(8,128)(2,1)S(1)}) custom-call(s32[2]{0:T(128)S(1)} %get-tuple-element.199.refs_0_, bf16[1024,512]{1,0:T(8,128)(2,1)S(1)} %get-tuple-element.160.refs_1_.refs_2_, bf16[1024,512]{1,0:T(8,128)(2,1)S(1)} %get-tuple-element.160.refs_1_.refs_2_, bf16[512,4096]{1,0:T(8,128)(2,1)} %refs_3_.15, ...), custom_call_target="tpu_custom_call" | custom-call | flops 1048576 | bytes 65536 | tf_op jit(solution)/shard_map/pallas_call | solution.py:333
  158.3 1.7 collective-permute-start.21
  160.0 3.3 %collective-permute-done.22.refs_4_ = bf16[64,4096]{1,0:T(8,128)(2,1)S(1)} collective-permute-done((bf16[64,4096]{1,0:T(8,128)(2,1)S(1)}, bf16[64,4096]{1,0:T(8,128)(2,1)S(1)}, u32[]{:S(2)}, u32[]{:S(2)}) %collective-permute-start.22) | collective-permute-done | bytes 524320 | tf_op jit(solution)/shard_map/ppermute | solution.py:420
  163.3 1.7 collective-permute-done.23.refs_5_
  165.0 4.1 %shard_map.131 = (bf16[64,4096]{1,0:T(8,128)(2,1)S(1)}, bf16[64,4096]{1,0:T(8,128)(2,1)S(1)}) custom-call(s32[2]{0:T(128)S(1)} %get-tuple-element.193.refs_0_, bf16[1024,512]{1,0:T(8,128)(2,1)S(1)} %get-tuple-element.160.refs_1_.refs_2_, bf16[1024,512]{1,0:T(8,128)(2,1)S(1)} %get-tuple-element.160.refs_1_.refs_2_, bf16[512,4096]{1,0:T(8,128)(2,1)} %refs_3_.15, ...), custom_call_target="tpu_custom_call" | custom-call | flops 1048576 | bytes 65536 | tf_op jit(solution)/shard_map/pallas_call | solution.py:333
  169.6 1.7 collective-permute-start.25
  171.2 3.3 %collective-permute-done.20 = bf16[64,4096]{1,0:T(8,128)(2,1)S(1)} collective-permute-done((bf16[64,4096]{1,0:T(8,128)(2,1)S(1)}, bf16[64,4096]{1,0:T(8,128)(2,1)S(1)}, u32[]{:S(2)}, u32[]{:S(2)}) %collective-permute-start.20) | collective-permute-done | bytes 524320 | tf_op jit(solution)/shard_map/ppermute | solution.py:420
  174.5 1.7 collective-permute-done.21
  176.2 7.3 %collective-permute-done.24.refs_4_ = bf16[64,4096]{1,0:T(8,128)(2,1)S(1)} collective-permute-done((bf16[64,4096]{1,0:T(8,128)(2,1)S(1)}, bf16[64,4096]{1,0:T(8,128)(2,1)S(1)}, u32[]{:S(2)}, u32[]{:S(2)}) %collective-permute-start.24) | collective-permute-done | bytes 524320 | tf_op jit(solution)/shard_map/ppermute | solution.py:420
  183.6 1.6 collective-permute-done.25.refs_5_
  185.2 4.1 %shard_map.132 = (bf16[64,4096]{1,0:T(8,128)(2,1)S(1)}, bf16[64,4096]{1,0:T(8,128)(2,1)S(1)}) custom-call(s32[2]{0:T(128)S(1)} %get-tuple-element.194.refs_0_, bf16[1024,512]{1,0:T(8,128)(2,1)S(1)} %get-tuple-element.160.refs_1_.refs_2_, bf16[1024,512]{1,0:T(8,128)(2,1)S(1)} %get-tuple-element.160.refs_1_.refs_2_, bf16[512,4096]{1,0:T(8,128)(2,1)} %refs_3_.15, ...), custom_call_target="tpu_custom_call" | custom-call | flops 1048576 | bytes 65536 | tf_op jit(solution)/shard_map/pallas_call | solution.py:333
  189.7 1.8 collective-permute-start.27
  192.8 4.1 %shard_map.133 = (bf16[64,4096]{1,0:T(8,128)(2,1)S(1)}, bf16[64,4096]{1,0:T(8,128)(2,1)S(1)}) custom-call(s32[2]{0:T(128)S(1)} %pad_add_fusion.1.refs_0_, bf16[1024,512]{1,0:T(8,128)(2,1)S(1)} %get-tuple-element.160.refs_1_.refs_2_, bf16[1024,512]{1,0:T(8,128)(2,1)S(1)} %get-tuple-element.160.refs_1_.refs_2_, bf16[512,4096]{1,0:T(8,128)(2,1)} %refs_3_.15), custom_call_target="tpu_custom_call" | custom-call | flops 1048576 | bytes 65536 | tf_op jit(solution)/shard_map/pallas_call | solution.py:333
  196.9 4.3 %collective-permute-done.26 = bf16[64,4096]{1,0:T(8,128)(2,1)} collective-permute-done((bf16[64,4096]{1,0:T(8,128)(2,1)S(1)}, bf16[64,4096]{1,0:T(8,128)(2,1)}, u32[]{:S(2)}, u32[]{:S(2)}) %collective-permute-start.26) | collective-permute-done | bytes 524320 | tf_op jit(solution)/shard_map/ppermute | solution.py:423
  201.3 1.6 convert_add_fusion.1
  203.0 1.2 fusion.2
  (93 shorter events, 15.0 us)
Async XLA Ops:
  0.0 15.0 %slice-start = ((bf16[4096,256]{1,0:T(8,128)(2,1)}), bf16[4096,128]{1,0:T(8,128)(2,1)S(1)}, s32[]{:S(2)}) async-start(bf16[4096,256]{1,0:T(8,128)(2,1)} %refs_10_.13), calls=%async_computation | async-start | bytes 2097152 | tf_op jit(solution)/shard_map/slice | solution.py:374
  2.4 29.1 %collective-permute-start.3 = (bf16[64,4096]{1,0:T(8,128)(2,1)}, bf16[64,4096]{1,0:T(8,128)(2,1)}, u32[]{:S(2)}, u32[]{:S(2)}) collective-permute-start(bf16[64,4096]{1,0:T(8,128)(2,1)} %get-tuple-element.203), channel_id=1, source_target_pairs={{2,0},{4,2},{6,4},{7,6},{5,7},{3,5},{1,3},{0,1},{10,8},{12,10},{14... | collective-permute-start | bytes 1572872 | tf_op jit(solution)/shard_map/ppermute | solution.py:423
  5.3 36.8 %collective-permute-start = (bf16[64,4096]{1,0:T(8,128)(2,1)}, bf16[64,4096]{1,0:T(8,128)(2,1)S(1)}, u32[]{:S(2)}, u32[]{:S(2)}) collective-permute-start(bf16[64,4096]{1,0:T(8,128)(2,1)} %get-tuple-element.203), channel_id=1, source_target_pairs={{0,2},{2,4},{4,6},{6,7},{7,5},{5,3},{3,1},{1,0},{8,10},{10,12},{12... | collective-permute-start | bytes 1572872 | tf_op jit(solution)/shard_map/ppermute | solution.py:420
  5.4 26.0 %collective-permute-start.2 = (bf16[64,4096]{1,0:T(8,128)(2,1)}, bf16[64,4096]{1,0:T(8,128)(2,1)}, u32[]{:S(2)}, u32[]{:S(2)}) collective-permute-start(bf16[64,4096]{1,0:T(8,128)(2,1)} %get-tuple-element.202), channel_id=1, source_target_pairs={{0,2},{2,4},{4,6},{6,7},{7,5},{5,3},{3,1},{1,0},{8,10},{10,12},{12... | collective-permute-start | bytes 1572872 | tf_op jit(solution)/shard_map/ppermute | solution.py:420
  7.4 34.7 %collective-permute-start.1 = (bf16[64,4096]{1,0:T(8,128)(2,1)}, bf16[64,4096]{1,0:T(8,128)(2,1)S(1)}, u32[]{:S(2)}, u32[]{:S(2)}) collective-permute-start(bf16[64,4096]{1,0:T(8,128)(2,1)} %get-tuple-element.202), channel_id=1, source_target_pairs={{2,0},{4,2},{6,4},{7,6},{5,7},{3,5},{1,3},{0,1},{10,8},{12,10},{14... | collective-permute-start | bytes 1572872 | tf_op jit(solution)/shard_map/ppermute | solution.py:423
  16.8 3.3 %copy-start.6 = (bf16[4096]{0:T(1024)(128)(2,1)S(1)}, bf16[4096]{0:T(1024)(128)(2,1)}, u32[]{:S(2)}) copy-start(bf16[4096]{0:T(1024)(128)(2,1)} %param.13) | copy-start | bytes 24580
  16.8 5.4 %copy-start.5 = (s32[1024]{0:T(1024)S(1)}, s32[1024]{0:T(1024)}, u32[]{:S(2)}) copy-start(s32[1024]{0:T(1024)} %param.18) | copy-start | bytes 12292
  16.9 5.7 %copy-start = (bf16[128,4096]{1,0:T(8,128)(2,1)S(1)}, bf16[128,4096]{1,0:T(8,128)(2,1)}, u32[]{:S(2)}) copy-start(bf16[128,4096]{1,0:T(8,128)(2,1)} %refs_2_.1) | copy-start | bytes 3145732
  31.4 23.1 %collective-permute-start.6 = (bf16[64,4096]{1,0:T(8,128)(2,1)}, bf16[64,4096]{1,0:T(8,128)(2,1)S(1)}, u32[]{:S(2)}, u32[]{:S(2)}) collective-permute-start(bf16[64,4096]{1,0:T(8,128)(2,1)} %collective-permute-done.2.refs_2_), channel_id=1, source_target_pairs={{0,2},{2,4},{4,6},{6,7},{7,5},{5,3},{3,1},{1,0},{8,10},{10,12},{12... | collective-permute-start | bytes 1572872 | tf_op jit(solution)/shard_map/ppermute | solution.py:420
  31.5 23.0 %collective-permute-start.7 = (bf16[64,4096]{1,0:T(8,128)(2,1)}, bf16[64,4096]{1,0:T(8,128)(2,1)S(1)}, u32[]{:S(2)}, u32[]{:S(2)}) collective-permute-start(bf16[64,4096]{1,0:T(8,128)(2,1)} %collective-permute-done.3.refs_3_), channel_id=1, source_target_pairs={{2,0},{4,2},{6,4},{7,6},{5,7},{3,5},{1,3},{0,1},{10,8},{12,10},{14... | collective-permute-start | bytes 1572872 | tf_op jit(solution)/shard_map/ppermute | solution.py:423
  42.1 21.3 %collective-permute-start.4 = (bf16[64,4096]{1,0:T(8,128)(2,1)S(1)}, bf16[64,4096]{1,0:T(8,128)(2,1)S(1)}, u32[]{:S(2)}, u32[]{:S(2)}) collective-permute-start(bf16[64,4096]{1,0:T(8,128)(2,1)S(1)} %collective-permute-done.refs_2_), channel_id=1, source_target_pairs={{0,2},{2,4},{4,6},{6,7},{7,5},{5,3},{3,1},{1,0},{8,10},{10,12},{12... | collective-permute-start | bytes 1572872 | tf_op jit(solution)/shard_map/ppermute | solution.py:420
  42.2 21.2 %collective-permute-start.5 = (bf16[64,4096]{1,0:T(8,128)(2,1)S(1)}, bf16[64,4096]{1,0:T(8,128)(2,1)S(1)}, u32[]{:S(2)}, u32[]{:S(2)}) collective-permute-start(bf16[64,4096]{1,0:T(8,128)(2,1)S(1)} %collective-permute-done.1.refs_3_), channel_id=1, source_target_pairs={{2,0},{4,2},{6,4},{7,6},{5,7},{3,5},{1,3},{0,1},{10,8},{12,10},{14... | collective-permute-start | bytes 1572872 | tf_op jit(solution)/shard_map/ppermute | solution.py:423
  54.5 22.5 %collective-permute-start.10 = (bf16[64,4096]{1,0:T(8,128)(2,1)S(1)}, bf16[64,4096]{1,0:T(8,128)(2,1)S(1)}, u32[]{:S(2)}, u32[]{:S(2)}) collective-permute-start(bf16[64,4096]{1,0:T(8,128)(2,1)S(1)} %collective-permute-done.6.refs_2_), channel_id=1, source_target_pairs={{0,2},{2,4},{4,6},{6,7},{7,5},{5,3},{3,1},{1,0},{8,10},{10,12},{12... | collective-permute-start | bytes 1572872 | tf_op jit(solution)/shard_map/ppermute | solution.py:420
  55.5 21.6 %collective-permute-start.11 = (bf16[64,4096]{1,0:T(8,128)(2,1)S(1)}, bf16[64,4096]{1,0:T(8,128)(2,1)S(1)}, u32[]{:S(2)}, u32[]{:S(2)}) collective-permute-start(bf16[64,4096]{1,0:T(8,128)(2,1)S(1)} %collective-permute-done.7.refs_3_), channel_id=1, source_target_pairs={{2,0},{4,2},{6,4},{7,6},{5,7},{3,5},{1,3},{0,1},{10,8},{12,10},{14... | collective-permute-start | bytes 1572872 | tf_op jit(solution)/shard_map/ppermute | solution.py:423
  63.5 23.1 %collective-permute-start.8 = (bf16[64,4096]{1,0:T(8,128)(2,1)S(1)}, bf16[64,4096]{1,0:T(8,128)(2,1)S(1)}, u32[]{:S(2)}, u32[]{:S(2)}) collective-permute-start(bf16[64,4096]{1,0:T(8,128)(2,1)S(1)} %collective-permute-done.4.refs_2_), channel_id=1, source_target_pairs={{0,2},{2,4},{4,6},{6,7},{7,5},{5,3},{3,1},{1,0},{8,10},{10,12},{12... | collective-permute-start | bytes 1572872 | tf_op jit(solution)/shard_map/ppermute | solution.py:420
  64.4 22.2 %collective-permute-start.9 = (bf16[64,4096]{1,0:T(8,128)(2,1)S(1)}, bf16[64,4096]{1,0:T(8,128)(2,1)S(1)}, u32[]{:S(2)}, u32[]{:S(2)}) collective-permute-start(bf16[64,4096]{1,0:T(8,128)(2,1)S(1)} %collective-permute-done.5.refs_3_), channel_id=1, source_target_pairs={{2,0},{4,2},{6,4},{7,6},{5,7},{3,5},{1,3},{0,1},{10,8},{12,10},{14... | collective-permute-start | bytes 1572872 | tf_op jit(solution)/shard_map/ppermute | solution.py:423
  77.1 25.2 %collective-permute-start.12 = (bf16[64,4096]{1,0:T(8,128)(2,1)S(1)}, bf16[64,4096]{1,0:T(8,128)(2,1)S(1)}, u32[]{:S(2)}, u32[]{:S(2)}) collective-permute-start(bf16[64,4096]{1,0:T(8,128)(2,1)S(1)} %collective-permute-done.10.refs_2_), channel_id=1, source_target_pairs={{0,2},{2,4},{4,6},{6,7},{7,5},{5,3},{3,1},{1,0},{8,10},{10,12},{12... | collective-permute-start | bytes 1572872 | tf_op jit(solution)/shard_map/ppermute | solution.py:420
  77.4 24.9 %collective-permute-start.13 = (bf16[64,4096]{1,0:T(8,128)(2,1)S(1)}, bf16[64,4096]{1,0:T(8,128)(2,1)S(1)}, u32[]{:S(2)}, u32[]{:S(2)}) collective-permute-start(bf16[64,4096]{1,0:T(8,128)(2,1)S(1)} %collective-permute-done.11.refs_3_), channel_id=1, source_target_pairs={{2,0},{4,2},{6,4},{7,6},{5,7},{3,5},{1,3},{0,1},{10,8},{12,10},{14... | collective-permute-start | bytes 1572872 | tf_op jit(solution)/shard_map/ppermute | solution.py:423
  102.3 15.4 %collective-permute-start.14 = (bf16[64,4096]{1,0:T(8,128)(2,1)S(1)}, bf16[64,4096]{1,0:T(8,128)(2,1)S(1)}, u32[]{:S(2)}, u32[]{:S(2)}) collective-permute-start(bf16[64,4096]{1,0:T(8,128)(2,1)S(1)} %get-tuple-element.152), channel_id=1, source_target_pairs={{0,2},{2,4},{4,6},{6,7},{7,5},{5,3},{3,1},{1,0},{8,10},{10,12},{12... | collective-permute-start | bytes 1572872 | tf_op jit(solution)/shard_map/ppermute | solution.py:420
  108.2 13.6 %collective-permute-start.15 = (bf16[64,4096]{1,0:T(8,128)(2,1)S(1)}, bf16[64,4096]{1,0:T(8,128)(2,1)S(1)}, u32[]{:S(2)}, u32[]{:S(2)}) collective-permute-start(bf16[64,4096]{1,0:T(8,128)(2,1)S(1)} %get-tuple-element.153), channel_id=1, source_target_pairs={{2,0},{4,2},{6,4},{7,6},{5,7},{3,5},{1,3},{0,1},{10,8},{12,10},{14... | collective-permute-start | bytes 1572872 | tf_op jit(solution)/shard_map/ppermute | solution.py:423
  125.9 14.9 %collective-permute-start.18 = (bf16[64,4096]{1,0:T(8,128)(2,1)S(1)}, bf16[64,4096]{1,0:T(8,128)(2,1)S(1)}, u32[]{:S(2)}, u32[]{:S(2)}) collective-permute-start(bf16[64,4096]{1,0:T(8,128)(2,1)S(1)} %get-tuple-element.163), channel_id=1, source_target_pairs={{0,2},{2,4},{4,6},{6,7},{7,5},{5,3},{3,1},{1,0},{8,10},{10,12},{12... | collective-permute-start | bytes 1572872 | tf_op jit(solution)/shard_map/ppermute | solution.py:420
  127.7 14.9 %collective-permute-start.19 = (bf16[64,4096]{1,0:T(8,128)(2,1)S(1)}, bf16[64,4096]{1,0:T(8,128)(2,1)S(1)}, u32[]{:S(2)}, u32[]{:S(2)}) collective-permute-start(bf16[64,4096]{1,0:T(8,128)(2,1)S(1)} %get-tuple-element.164), channel_id=1, source_target_pairs={{2,0},{4,2},{6,4},{7,6},{5,7},{3,5},{1,3},{0,1},{10,8},{12,10},{14... | collective-permute-start | bytes 1572872 | tf_op jit(solution)/shard_map/ppermute | solution.py:423
  132.1 19.9 %collective-permute-start.16 = (bf16[64,4096]{1,0:T(8,128)(2,1)S(1)}, bf16[64,4096]{1,0:T(8,128)(2,1)S(1)}, u32[]{:S(2)}, u32[]{:S(2)}) collective-permute-start(bf16[64,4096]{1,0:T(8,128)(2,1)S(1)} %get-tuple-element.167), channel_id=1, source_target_pairs={{0,2},{2,4},{4,6},{6,7},{7,5},{5,3},{3,1},{1,0},{8,10},{10,12},{12... | collective-permute-start | bytes 1572872 | tf_op jit(solution)/shard_map/ppermute | solution.py:420
  133.9 19.9 %collective-permute-start.17 = (bf16[64,4096]{1,0:T(8,128)(2,1)S(1)}, bf16[64,4096]{1,0:T(8,128)(2,1)S(1)}, u32[]{:S(2)}, u32[]{:S(2)}) collective-permute-start(bf16[64,4096]{1,0:T(8,128)(2,1)S(1)} %get-tuple-element.168), channel_id=1, source_target_pairs={{2,0},{4,2},{6,4},{7,6},{5,7},{3,5},{1,3},{0,1},{10,8},{12,10},{14... | collective-permute-start | bytes 1572872 | tf_op jit(solution)/shard_map/ppermute | solution.py:423
  146.7 16.6 %collective-permute-start.22 = (bf16[64,4096]{1,0:T(8,128)(2,1)S(1)}, bf16[64,4096]{1,0:T(8,128)(2,1)S(1)}, u32[]{:S(2)}, u32[]{:S(2)}) collective-permute-start(bf16[64,4096]{1,0:T(8,128)(2,1)S(1)} %get-tuple-element.171), channel_id=1, source_target_pairs={{0,2},{2,4},{4,6},{6,7},{7,5},{5,3},{3,1},{1,0},{8,10},{10,12},{12... | collective-permute-start | bytes 1572872 | tf_op jit(solution)/shard_map/ppermute | solution.py:420
  147.1 17.9 %collective-permute-start.23 = (bf16[64,4096]{1,0:T(8,128)(2,1)S(1)}, bf16[64,4096]{1,0:T(8,128)(2,1)S(1)}, u32[]{:S(2)}, u32[]{:S(2)}) collective-permute-start(bf16[64,4096]{1,0:T(8,128)(2,1)S(1)} %get-tuple-element.172), channel_id=1, source_target_pairs={{2,0},{4,2},{6,4},{7,6},{5,7},{3,5},{1,3},{0,1},{10,8},{12,10},{14... | collective-permute-start | bytes 1572872 | tf_op jit(solution)/shard_map/ppermute | solution.py:423
  157.9 16.6 %collective-permute-start.20 = (bf16[64,4096]{1,0:T(8,128)(2,1)S(1)}, bf16[64,4096]{1,0:T(8,128)(2,1)S(1)}, u32[]{:S(2)}, u32[]{:S(2)}) collective-permute-start(bf16[64,4096]{1,0:T(8,128)(2,1)S(1)} %get-tuple-element.175), channel_id=1, source_target_pairs={{0,2},{2,4},{4,6},{6,7},{7,5},{5,3},{3,1},{1,0},{8,10},{10,12},{12... | collective-permute-start | bytes 1572872 | tf_op jit(solution)/shard_map/ppermute | solution.py:420
  158.3 17.9 %collective-permute-start.21 = (bf16[64,4096]{1,0:T(8,128)(2,1)S(1)}, bf16[64,4096]{1,0:T(8,128)(2,1)S(1)}, u32[]{:S(2)}, u32[]{:S(2)}) collective-permute-start(bf16[64,4096]{1,0:T(8,128)(2,1)S(1)} %get-tuple-element.176), channel_id=1, source_target_pairs={{2,0},{4,2},{6,4},{7,6},{5,7},{3,5},{1,3},{0,1},{10,8},{12,10},{14... | collective-permute-start | bytes 1572872 | tf_op jit(solution)/shard_map/ppermute | solution.py:423
  169.2 14.4 %collective-permute-start.24 = (bf16[64,4096]{1,0:T(8,128)(2,1)S(1)}, bf16[64,4096]{1,0:T(8,128)(2,1)S(1)}, u32[]{:S(2)}, u32[]{:S(2)}) collective-permute-start(bf16[64,4096]{1,0:T(8,128)(2,1)S(1)} %get-tuple-element.179), channel_id=1, source_target_pairs={{0,2},{2,4},{4,6},{6,7},{7,5},{5,3},{3,1},{1,0},{8,10},{10,12},{12... | collective-permute-start | bytes 1572872 | tf_op jit(solution)/shard_map/ppermute | solution.py:420
  169.6 15.7 %collective-permute-start.25 = (bf16[64,4096]{1,0:T(8,128)(2,1)S(1)}, bf16[64,4096]{1,0:T(8,128)(2,1)S(1)}, u32[]{:S(2)}, u32[]{:S(2)}) collective-permute-start(bf16[64,4096]{1,0:T(8,128)(2,1)S(1)} %get-tuple-element.180), channel_id=1, source_target_pairs={{2,0},{4,2},{6,4},{7,6},{5,7},{3,5},{1,3},{0,1},{10,8},{12,10},{14... | collective-permute-start | bytes 1572872 | tf_op jit(solution)/shard_map/ppermute | solution.py:423
  174.5 14.9 %copy-start.1 = (bf16[64,4096]{1,0:T(8,128)(2,1)}, bf16[64,4096]{1,0:T(8,128)(2,1)S(1)}, u32[]{:S(2)}) copy-start(bf16[64,4096]{1,0:T(8,128)(2,1)S(1)} %collective-permute-done.20) | copy-start | bytes 1572868
  176.2 13.2 %copy-start.3 = (bf16[64,4096]{1,0:T(8,128)(2,1)}, bf16[64,4096]{1,0:T(8,128)(2,1)S(1)}, u32[]{:S(2)}) copy-start(bf16[64,4096]{1,0:T(8,128)(2,1)S(1)} %collective-permute-done.21) | copy-start | bytes 1572868
  185.2 6.3 %copy-start.7 = (s32[8]{0:T(128)S(1)}, s32[8]{0:T(128)}, u32[]{:S(2)}) copy-start(s32[8]{0:T(128)} %constant.79.clone) | copy-start | bytes 100
  189.4 11.9 %collective-permute-start.26 = (bf16[64,4096]{1,0:T(8,128)(2,1)S(1)}, bf16[64,4096]{1,0:T(8,128)(2,1)}, u32[]{:S(2)}, u32[]{:S(2)}) collective-permute-start(bf16[64,4096]{1,0:T(8,128)(2,1)S(1)} %get-tuple-element.188), channel_id=1, source_target_pairs={{2,0},{4,2},{6,4},{7,6},{5,7},{3,5},{1,3},{0,1},{10,8},{12,10},{14... | collective-permute-start | bytes 1572872 | tf_op jit(solution)/shard_map/ppermute | solution.py:423
  189.7 11.6 %collective-permute-start.27 = (bf16[64,4096]{1,0:T(8,128)(2,1)S(1)}, bf16[64,4096]{1,0:T(8,128)(2,1)}, u32[]{:S(2)}, u32[]{:S(2)}) collective-permute-start(bf16[64,4096]{1,0:T(8,128)(2,1)S(1)} %get-tuple-element.187), channel_id=1, source_target_pairs={{0,2},{2,4},{4,6},{6,7},{7,5},{5,3},{3,1},{1,0},{8,10},{10,12},{12... | collective-permute-start | bytes 1572872 | tf_op jit(solution)/shard_map/ppermute | solution.py:420
  192.8 8.5 %copy-start.2 = (bf16[64,4096]{1,0:T(8,128)(2,1)S(1)}, bf16[64,4096]{1,0:T(8,128)(2,1)}, u32[]{:S(2)}) copy-start(bf16[64,4096]{1,0:T(8,128)(2,1)} %copy-done.1) | copy-start | bytes 1572868
  192.8 8.5 %copy-start.4 = (bf16[64,4096]{1,0:T(8,128)(2,1)S(1)}, bf16[64,4096]{1,0:T(8,128)(2,1)}, u32[]{:S(2)}) copy-start(bf16[64,4096]{1,0:T(8,128)(2,1)} %copy-done.3) | copy-start | bytes 1572868
